TPU v7x, 256 devices: a whole 4x4x8 slice. The times are simulated.
256 devices in a mesh: ctx: 32 (over y, z_hi, core), tp: 8 (over x, z_lo).
Axes of the slice: x: 4, y: 4, z: 8 (z_hi: 4, z_lo: 2; z = z_hi * 2 + z_lo), core: 2. Of those that a mesh axis runs over, the one named last changes fastest.
Arguments:
- tokens: bfloat16 [16384, 2560], P('ctx'), may hold values from -6 to 6
- inner_weight: bfloat16 [2560, 5120], P(None, 'tp'), may hold values from -0.125 to 0.125
- shared_weight: bfloat16 [2560, 256], replicated, may hold values from -0.125 to 0.125
- step_weight: bfloat16 [2560, 80], P(None, 'tp'), may hold values from -0.125 to 0.125
- conv_inner: float32 [4, 5120], P(None, 'tp'), may hold values from -3 to 3
- conv_shared: float32 [4, 256], replicated, may hold values from -0.375 to 0.375
- step_bias: float32 [80], P('tp'), may hold values from -2 to 1
- decay_rate: float32 [80], P('tp'), may hold values from 0 to 0.06, as said below
- skip_gain: float32 [80], P('tp'), may hold values from 0.5 to 1.5
- cotangent: bfloat16 [16384, 5120], P('ctx', 'tp'), may hold values from -6 to 6
Outputs:
- mixed: bfloat16 [16384, 5120], P('ctx', 'tp')
- grad_tokens: bfloat16 [16384, 2560], P('ctx', 'tp')
- grad_inner_weight: float32 [2560, 5120], P('ctx', 'tp')
- grad_shared_weight: float32 [2560, 256], P('ctx', 'tp')
- grad_step_weight: float32 [2560, 80], P('ctx', 'tp')
Inputs may be any that keep to these rules, and one draw needn't show every extreme that they name: `decay_rate`: decay rates are positive.
All inputs are finite; a program needn't handle non-finite values.
Results may differ from a plain program's by a relative error of at most 0.0031.
Values sent between devices are 32-bit elements; how exact they have to be, the bound alone decides.
No kernel may reach another device: no remote copies, remote signals or barrier semaphores. Data moves between devices by JAX's collectives and lax.ppermute only.
A program may use at most 192 MiB of HBM per device.

v0:
```python
import jax
import jax.numpy as jnp
from jax import lax
from jax.sharding import PartitionSpec as P

P_SIZE = 64
N = 128
K = 4
GROUP = 256


def from_behind(block, axis, distance):
    devices = range(lax.axis_size(axis))
    route = [(i - distance, i) for i in devices if i - distance in devices]
    return lax.ppermute(block, axis, route)


def group_terms(values, b_vectors, c_vectors, step_size, decay_rate, skip_gain):
    log_decay = -decay_rate[None, :] * step_size
    cum_logs = jnp.cumsum(log_decay, 0)
    length = step_size.shape[0]
    causal = (jnp.arange(length)[:, None] >= jnp.arange(length)[None, :])[:, :, None]
    log_gaps = cum_logs[:, None, :] - cum_logs[None, :, :]
    decays = jnp.where(causal, jnp.exp(jnp.where(causal, log_gaps, 0.0)), 0.0)
    scores = jnp.dot(c_vectors, b_vectors.T, precision=lax.Precision.HIGHEST)
    weights = scores[:, :, None] * decays * step_size[None, :, :]
    inside = jnp.einsum("ijh,jhp->ihp", weights, values, precision=lax.Precision.HIGHEST)
    inside = inside + skip_gain[None, :, None] * values
    tail_weight = jnp.exp(cum_logs[-1][None, :] - cum_logs) * step_size
    written = jnp.einsum(
        "jh,jhp,jn->hpn", tail_weight, values, b_vectors, precision=lax.Precision.HIGHEST
    )
    return (inside, cum_logs, written)


def local_mixer(pre_ext, step_pre, conv_taps, step_bias, decay_rate, skip_gain):
    length = step_pre.shape[0]
    heads_here = step_pre.shape[1]
    inner = heads_here * P_SIZE
    blocks_count = length // GROUP
    conv_out = jnp.zeros((length, pre_ext.shape[1]), jnp.float32)
    for offset in range(K):
        conv_out = conv_out + conv_taps[offset][None, :] * pre_ext[offset : offset + length]
    active = jax.nn.silu(conv_out)
    values = active[:, :inner].reshape(blocks_count, GROUP, heads_here, P_SIZE)
    b_vectors = active[:, inner : inner + N].reshape(blocks_count, GROUP, N)
    c_flat = active[:, inner + N :]
    c_vectors = c_flat.reshape(blocks_count, GROUP, N)
    step_size = jax.nn.softplus(step_pre + step_bias[None, :]).reshape(
        blocks_count, GROUP, heads_here
    )

    def advance(carry, blocks):
        memory, log_total = carry
        values_b, b_block, c_block, step_block = blocks
        inside, cum_logs, written = group_terms(
            values_b, b_block, c_block, step_block, decay_rate, skip_gain
        )
        carried = jnp.einsum("in,hpn->ihp", c_block, memory, precision=lax.Precision.HIGHEST)
        carried = carried * jnp.exp(cum_logs)[:, :, None]
        fresh = jnp.exp(cum_logs[-1])[:, None, None] * memory + written
        read_decay = jnp.exp(cum_logs + log_total[None, :])
        return ((fresh, log_total + cum_logs[-1]), (inside + carried, read_decay))

    start_carry = (
        jnp.zeros((heads_here, P_SIZE, N), jnp.float32),
        jnp.zeros((heads_here,), jnp.float32),
    )
    (memory, log_total), (outputs, read_decay) = lax.scan(
        advance, start_carry, (values, b_vectors, c_vectors, step_size)
    )
    return (
        outputs.reshape(length, heads_here, P_SIZE),
        memory,
        log_total,
        read_decay.reshape(length, heads_here),
        c_flat,
    )


def forward_combine(earlier, later):
    return (earlier[0] + later[0], jnp.exp(later[0])[:, None, None] * earlier[1] + later[1])


def backward_combine(earlier, later):
    return (later[0] + earlier[0], later[1] + jnp.exp(later[0])[:, None, None] * earlier[1])


def forward_hops(own, identity):

    def forward_one_turn(turn, carry):
        upto, received = carry
        incoming = from_behind(upto, "ctx", 1)
        return (forward_combine(incoming, own), incoming)

    final = lax.fori_loop(0, lax.axis_size("ctx") - 1, forward_one_turn, (own, identity))
    return final[1]


def backward_hops(own, identity):

    def backward_one_turn(turn, carry):
        upto, received = carry
        incoming = from_behind(upto, "ctx", -1)
        return (backward_combine(incoming, own), incoming)

    final = lax.fori_loop(0, lax.axis_size("ctx") - 1, backward_one_turn, (own, identity))
    return final[1]


def body(
    tokens,
    inner_weight,
    shared_weight,
    step_weight,
    conv_inner,
    conv_shared,
    step_bias,
    decay_rate,
    skip_gain,
    cotangent,
):
    length = tokens.shape[0]
    inner = inner_weight.shape[1]
    heads_here = step_weight.shape[1]
    inner_pre = jnp.dot(tokens, inner_weight, preferred_element_type=jnp.float32)
    shared_pre = jnp.dot(tokens, shared_weight, preferred_element_type=jnp.float32)
    step_pre = jnp.dot(tokens, step_weight, preferred_element_type=jnp.float32)
    pre = jnp.concatenate([inner_pre, shared_pre], 1)
    rim_rows = from_behind(pre[length - (K - 1) :], "ctx", 1)
    pre_ext = jnp.concatenate([rim_rows, pre], 0)
    conv_taps = jnp.concatenate([conv_inner, conv_shared], 1)

    def mixer_local(pre_part, step_part):
        return local_mixer(pre_part, step_part, conv_taps, step_bias, decay_rate, skip_gain)

    (local_out, sent_state, log_total, read_decay, c_flat), pullback = jax.vjp(
        mixer_local, pre_ext, step_pre
    )
    grad_mixed = cotangent.astype(jnp.float32).reshape(length, heads_here, P_SIZE)
    own_grad = jnp.einsum(
        "th,thp,tn->hpn", read_decay, grad_mixed, c_flat, precision=lax.Precision.HIGHEST
    )
    identity = (jnp.zeros_like(log_total), jnp.zeros_like(sent_state))
    arrived = forward_hops((log_total, sent_state), identity)[1]
    later_grad = backward_hops((log_total, own_grad), identity)[1]
    from_before = jnp.einsum(
        "th,tn,hpn->thp", read_decay, c_flat, arrived, precision=lax.Precision.HIGHEST
    )
    mixed = (local_out + from_before).reshape(length, inner).astype(jnp.bfloat16)
    grad_log_total = jnp.sum(later_grad * arrived, (1, 2)) * jnp.exp(log_total)
    side_term = jnp.einsum("thp,hpn->thn", grad_mixed, arrived, precision=lax.Precision.HIGHEST)
    grad_read = jnp.einsum("thn,tn->th", side_term, c_flat, precision=lax.Precision.HIGHEST)
    grad_c_flat = jnp.einsum("th,thn->tn", read_decay, side_term, precision=lax.Precision.HIGHEST)
    grad_pre_ext, grad_step = pullback(
        (grad_mixed, later_grad, grad_log_total, grad_read, grad_c_flat)
    )
    rim_back = from_behind(grad_pre_ext[: K - 1], "ctx", -1)
    grad_pre = grad_pre_ext[K - 1 :] + jnp.pad(rim_back, ((length - (K - 1), 0), (0, 0)))
    grad_inner = grad_pre[:, :inner].astype(jnp.bfloat16)
    grad_shared = grad_pre[:, inner:]
    partial_tokens = jnp.dot(grad_inner, inner_weight.T, preferred_element_type=jnp.float32)
    partial_tokens = partial_tokens + jnp.dot(
        grad_shared, shared_weight.astype(jnp.float32).T, precision=lax.Precision.HIGHEST
    )
    partial_tokens = partial_tokens + jnp.dot(
        grad_step, step_weight.astype(jnp.float32).T, precision=lax.Precision.HIGHEST
    )
    token_share, shared_share = (
        lax.psum_scatter(partial_tokens, "tp", scatter_dimension=1, tiled=True),
        lax.psum_scatter(grad_shared, "tp", scatter_dimension=1, tiled=True),
    )
    shared_cols = shared_share.shape[1]
    segment_wide = tokens.astype(jnp.float32)
    first_part = jnp.dot(tokens.T, grad_inner, preferred_element_type=jnp.float32)
    second_part = jnp.dot(segment_wide.T, shared_share, precision=lax.Precision.HIGHEST)
    third_part = jnp.dot(segment_wide.T, grad_step, precision=lax.Precision.HIGHEST)
    summed = lax.psum_scatter(
        jnp.concatenate([first_part, second_part, third_part], 1),
        "ctx",
        scatter_dimension=0,
        tiled=True,
    )
    grad_inner_weight = summed[:, :inner]
    grad_shared_weight = summed[:, inner : inner + shared_cols]
    grad_step_weight = summed[:, inner + shared_cols :]
    return (
        mixed,
        token_share.astype(jnp.bfloat16),
        grad_inner_weight,
        grad_shared_weight,
        grad_step_weight,
    )


def solution(mesh):
    in_specs = (
        P("ctx", None),
        P(None, "tp"),
        P(),
        P(None, "tp"),
        P(None, "tp"),
        P(),
        P("tp"),
        P("tp"),
        P("tp"),
        P("ctx", "tp"),
    )
    out_specs = (P("ctx", "tp"), P("ctx", "tp"), P("ctx", "tp"), P("ctx", "tp"), P("ctx", "tp"))
    return jax.shard_map(body, mesh=mesh, in_specs=in_specs, out_specs=out_specs, check_vma=False)
```

profile of v0, /device:TPU:1, one launch (start us, length us, event | category | flops | bytes accessed | tf_op | source)
XLA Modules:
  0.0 1487.1 jit_solution(979875826855804953)
XLA Ops:
  49.6 105.9 %while.110 = (s32[]{:T(128)}, f32[10,64,128]{2,1,0:T(8,128)}, f32[10]{0:T(128)}, f32[2,256,10,64]{1,0,3,2:T(2,128)}, f32[2,256,10]{1,2,0:T(8,128)}, /*index=5*/f...) while((s32[]{:T(128)}, f32[10,64,128]{2,1,0:T(8,128)}, ...), condition=%wide.region_3.4_spmd.clone.clone, body=%wide.region_0.3_spmd.clone.clone.sunk | while | flops 1115580416 | bytes 30478348 | solution.py:69
  73.0 14.2 dynamic_update_slice.251
  125.1 14.2 dynamic_update_slice.251
  163.1 408.2 %while.107 = (s32[]{:T(128)}, f32[10,64,128]{2,1,0:T(8,128)}, f32[10,64,128]{2,1,0:T(8,128)}, f32[10,1,1]{0,2,1:T(1,128)S(1)}, f32[10,64,128]{2,1,0:T(8,128)}, /*index=5*/s32[]{:T(128)}) while((s32[]{:T(128)}, f32[10,64,128]{2,1,0:T(8,128)}, f32[10,64,128]{2,1,0:T(8,128)}, f32[10,1,1]{0,2,1:T(1,128)S(1)}, f32[10,64,128]{2,1,0:T(8,128)}, ...), condition=%wide.region_5.6_spmd, body=%wide.region_4.5_spmd.sunk | while | flops 163842 | bytes 2293909 | solution.py:96
  200.1 6.8 collective-permute-done
  214.1 7.8 collective-permute-done
  271.6 6.5 collective-permute-start
  581.3 420.0 %while.108 = (s32[]{:T(128)}, f32[10,64,128]{2,1,0:T(8,128)}, f32[10,64,128]{2,1,0:T(8,128)}, f32[10,1,1]{0,2,1:T(1,128)S(1)}, f32[10,64,128]{2,1,0:T(8,128)}, /*index=5*/s32[]{:T(128)}) while((s32[]{:T(128)}, f32[10,64,128]{2,1,0:T(8,128)}, f32[10,64,128]{2,1,0:T(8,128)}, f32[10,1,1]{0,2,1:T(1,128)S(1)}, f32[10,64,128]{2,1,0:T(8,128)}, ...), condition=%wide.region_7.8_spmd, body=%wide.region_6.7_spmd.sunk | while | flops 163842 | bytes 2293909 | solution.py:107
  583.4 8.5 collective-permute-done.1
  595.7 7.7 collective-permute-done.1
  607.2 9.5 collective-permute-done.1
  620.5 8.9 collective-permute-done.1
  633.2 8.9 collective-permute-done.1
  645.9 8.9 collective-permute-done.1
  658.6 8.9 collective-permute-done.1
  671.3 9.1 collective-permute-done.1
  684.2 11.1 collective-permute-done.1
  699.2 11.1 collective-permute-done.1
  714.1 11.1 collective-permute-done.1
  729.0 10.2 collective-permute-done.1
  743.0 9.9 collective-permute-done.1
  756.7 9.9 collective-permute-done.1
  770.4 9.9 collective-permute-done.1
  784.1 9.9 collective-permute-done.1
  797.8 9.9 collective-permute-done.1
  811.5 9.9 collective-permute-done.1
  825.2 9.9 collective-permute-done.1
  838.9 9.9 collective-permute-done.1
  852.6 9.9 collective-permute-done.1
  866.3 9.9 collective-permute-done.1
  880.0 9.9 collective-permute-done.1
  893.7 9.9 collective-permute-done.1
  907.4 9.9 collective-permute-done.1
  921.1 9.9 collective-permute-done.1
  934.8 9.9 collective-permute-done.1
  948.5 9.9 collective-permute-done.1
  962.1 9.9 collective-permute-done.1
  975.8 9.9 collective-permute-done.1
  989.5 9.9 collective-permute-done.1
  1006.8 142.5 %while.109 = (s32[]{:T(128)}, f32[10,64,128]{2,1,0:T(8,128)}, f32[10]{0:T(128)}, f32[2,256,10,64]{1,0,3,2:T(2,128)}, f32[2,256,128]{2,1,0:T(8,128)}, /*index=5*/...) while((s32[]{:T(128)}, f32[10,64,128]{2,1,0:T(8,128)}, ...), condition=%wide.region_20.21_spmd.clone.clone, body=%wide.region_9.20_spmd.clone.clone.sunk | while | flops 2224138752 | bytes 44093308 | solution.py:69
  1010.1 7.6 fusion.236
  1052.2 14.2 dynamic_update_slice.239
  1081.3 7.6 fusion.236
  1123.3 14.2 dynamic_update_slice.239
  1188.5 46.6 %reduce-scatter.10.cloned.1.call-done = f32[32,512]{1,0:T(8,128)} async-done(((f32[256,512]{1,0:T(8,128)}), f32[32,512]{1,0:T(8,128)}) %reduce-scatter.10.cloned.1.call-update) | async-done | bytes 65552
  1243.4 8.7 copy.161
  1261.3 92.6 %reduce-scatter.8.cloned.1.call-done = f32[512,320]{0,1:T(8,128)} async-done(((f32[512,2560]{0,1:T(8,128)}), f32[512,320]{0,1:T(8,128)}) %reduce-scatter.8.cloned.1.call-update) | async-done | bytes 655376 | tf_op jit(solution)/shard_map/reduce_scatter | solution.py:170
  1355.8 119.8 %reduce-scatter.12.cloned.1.call-done = f32[80,682]{1,0:T(8,128)} async-done(((f32[2560,682]{1,0:T(8,128)}), f32[80,682]{1,0:T(8,128)}) %reduce-scatter.12.cloned.1.call-update) | async-done | bytes 218256
  (525 shorter events, 808.5 us)
Async XLA Ops:
  7.2 1227.9 %reduce-scatter.10.cloned.1.call-start = ((), (), s32[]{:S(2)}) async-start(), calls=%async_computation.4 | async-start | bytes 589824
  14.3 18.0 %collective-permute-start.2 = (f32[3,896]{1,0:T(4,128)S(1)}, f32[3,896]{1,0:T(4,128)S(1)}, u32[]{:S(2)}, u32[]{:S(2)}) collective-permute-start(f32[3,896]{1,0:T(4,128)S(1)} %fusion.154), channel_id=1, source_target_pairs={{0,8},{8,16},{16,24},{24,32},{32,40},{40,48},{48,56},{56,64},{64,7... | collective-permute-start | bytes 32264 | tf_op jit(solution)/shard_map/ppermute | solution.py:15
  194.8 12.1 collective-permute-start
  208.8 13.2 collective-permute-start
  311.0 11.8 collective-permute-start
  324.8 11.8 collective-permute-start
  338.5 11.8 collective-permute-start
  352.2 11.8 collective-permute-start
  365.9 11.8 collective-permute-start
  379.6 11.8 collective-permute-start
  393.3 11.8 collective-permute-start
  407.0 11.8 collective-permute-start
  420.7 11.8 collective-permute-start
  434.4 11.8 collective-permute-start
  448.1 11.8 collective-permute-start
  461.8 11.8 collective-permute-start
  475.5 11.8 collective-permute-start
  489.2 11.8 collective-permute-start
  502.9 11.8 collective-permute-start
  516.6 11.8 collective-permute-start
  530.3 11.8 collective-permute-start
  544.0 11.8 collective-permute-start
  557.6 11.8 collective-permute-start
  682.3 13.1 collective-permute-start.1
  697.3 13.0 collective-permute-start.1
  712.2 13.0 collective-permute-start.1
  727.1 12.1 collective-permute-start.1
  741.0 11.8 collective-permute-start.1
  754.7 11.8 collective-permute-start.1
  768.4 11.8 collective-permute-start.1
  782.1 11.8 collective-permute-start.1
  795.8 11.8 collective-permute-start.1
  809.5 11.8 collective-permute-start.1
  823.2 11.8 collective-permute-start.1
  836.9 11.8 collective-permute-start.1
  850.6 11.8 collective-permute-start.1
  864.3 11.8 collective-permute-start.1
  878.0 11.8 collective-permute-start.1
  891.7 11.8 collective-permute-start.1
  905.4 11.8 collective-permute-start.1
  919.1 11.8 collective-permute-start.1
  932.8 11.8 collective-permute-start.1
  946.5 11.8 collective-permute-start.1
  960.2 11.8 collective-permute-start.1
  973.9 11.8 collective-permute-start.1
  987.6 11.8 collective-permute-start.1
  1170.3 183.6 %reduce-scatter.8.cloned.1.call-start = ((), (), s32[]{:S(2)}) async-start(), calls=%async_computation.3 | async-start | bytes 5898240 | tf_op jit(solution)/shard_map/reduce_scatter | solution.py:170
  1179.2 296.3 %reduce-scatter.12.cloned.1.call-start = ((), (), s32[]{:S(2)}) async-start(), calls=%async_computation.5 | async-start | bytes 8110080
  (90 other events, 1015.8 us)
Sparse Core Ops, SparseCore 0:
  1170.5 64.6 reduce-scatter.9
  1237.8 116.0 reduce-scatter.7
  1358.6 116.9 reduce-scatter.11
where the time goes:
time: 1500 us; the launch traced here: 1490 us
  waiting for transfers between devices  744 us (50%)
  starting transfers between devices  234 us (16%)
  other arithmetic  196 us (13%)
  local copies, waits for them, and re-layouts  186 us (12%)
  matrix products  111 us (7%)
    ppermute x64, waiting for transfers between devices, from_behind(): return lax.ppermute(block, axis, route)  485 us
    ppermute x64, starting transfers between devices, from_behind(): return lax.ppermute(block, axis, route)  234 us
    unnamed x5, waiting for transfers between devices  166 us
    reduce_scatter x1, waiting for transfers between devices, body(): lax.psum_scatter(partial_tokens, 'tp', scatter_dimension=1, tiled=True)  92.6 us
    dynamic_update_slice x22, local copies, waits for them, and re-layouts, local_mixer(): lax.scan(advance, start_carry, (values, b_vectors, c_vectors, step_size))  77.7 us
    add x31, other arithmetic, backward_combine(): later[1] + jnp.exp(later[0])[:, None, None] * earlier[1]  58.7 us
    add x31, other arithmetic, forward_combine(): jnp.exp(later[0])[:, None, None] * earlier[1] + later[1]  58.7 us
    dot_general x6, matrix products, group_terms(): jnp.einsum('ijh,jhp->ihp', weights, values, precision=lax.Precision.HIGHEST)  32.4 us
  transfers between devices with their start and end apart: 67, of which 65 were waited for; matrix products, arithmetic and copies ran while one was open for 4% of the time, Pallas kernels for 0%

commit v1 on v0

v1 whole, which is shorter than its diff:
```python
import functools

import jax
import jax.numpy as jnp
from jax import lax
from jax.experimental import pallas as pl
from jax.experimental.pallas import tpu as pltpu
from jax.sharding import PartitionSpec as P

P_SIZE = 64
N = 128
K = 4
LANES = 128
SLOT = 16
F32 = jnp.float32
BF16 = jnp.bfloat16
NN = (((1,), (0,)), ((), ()))
NT = (((1,), (1,)), ((), ()))
TN = (((0,), (0,)), ((), ()))
PARAMS = pltpu.CompilerParams(vmem_limit_bytes=48 * 1024 * 1024)


def shifted(block, axis, distance):
    size = lax.axis_size(axis)
    return lax.ppermute(block, axis, [(i, (i + distance) % size) for i in range(size)])


def dot1(a, b, dims):
    return lax.dot_general(a, b, dims, preferred_element_type=F32)


def split(a):
    high = a.astype(BF16)
    return high, (a - high.astype(F32)).astype(BF16)


def dot3(a, b, dims):
    ah, al = a
    bh, bl = b
    return dot1(ah, bh, dims) + (dot1(ah, bl, dims) + dot1(al, bh, dims))


def dot2(a, b, dims):
    return dot1(a[0], b, dims) + dot1(a[1], b, dims)


def sigmoid(z):
    return 1.0 / (1.0 + jnp.exp(-z))


def of_tile(cols, k):
    lane = lax.broadcasted_iota(jnp.int32, (cols.shape[0], LANES), 1)
    left = jnp.broadcast_to(cols[:, 2 * k : 2 * k + 1], lane.shape)
    right = jnp.broadcast_to(cols[:, 2 * k + 1 : 2 * k + 2], lane.shape)
    return jnp.where(lane < P_SIZE, left, right)


def triangle_sum(a, dims):
    length = a.shape[0]
    row = lax.broadcasted_iota(jnp.int32, (length, length), 0)
    col = lax.broadcasted_iota(jnp.int32, (length, length), 1)
    reach = row >= col if dims == NN else row <= col
    ones = jnp.where(reach, 1.0, 0.0).astype(BF16)
    first = a.astype(BF16).astype(F32)
    second = (a - first).astype(BF16).astype(F32)
    third = (a - first - second).astype(BF16).astype(F32)
    packed = first + pltpu.roll(second, SLOT, 1) + pltpu.roll(third, 2 * SLOT, 1)
    sums = dot1(ones, packed.astype(BF16), NN)
    total = sums + pltpu.roll(sums, LANES - SLOT, 1) + pltpu.roll(sums, LANES - 2 * SLOT, 1)
    lane = lax.broadcasted_iota(jnp.int32, total.shape, 1)
    return jnp.where(lane < SLOT, total, 0.0)


def project_kernel(
    tiles, heads,
    edge_ref, tok_ref, rim_ref, wi_ref, ws_ref, wt_ref, ci_ref, cs_ref, par_ref, cot_ref,
    z_ref, sp_ref, dt_ref, cum_ref, cumt_ref, pay_ref,
    lhs, acc_i, acc_s, acc_t,
):
    step = pl.program_id(0)
    length = tok_ref.shape[0]
    head_rows = lhs.shape[0] - length
    inner = wi_ref.shape[1]

    @pl.when(step == 0)
    def _():
        acc_i[...] = jnp.zeros_like(acc_i)
        acc_s[...] = jnp.zeros_like(acc_s)
        acc_t[...] = jnp.zeros_like(acc_t)

    keep = jnp.where(edge_ref[0] == 0, 0.0, 1.0)
    rim = rim_ref[...] * keep
    lhs[0:head_rows, :] = jnp.concatenate([jnp.zeros_like(rim), rim], 0).astype(BF16)
    lhs[head_rows:, :] = tok_ref[...]
    left = lhs[...]
    acc_i[...] += dot1(left, wi_ref[...], NN)
    acc_s[...] += dot1(left, ws_ref[...], NN)
    acc_t[:, 0:heads] += dot1(left, wt_ref[...], NN)

    @pl.when(step == pl.num_programs(0) - 1)
    def _():
        start = head_rows - (K - 1)
        sp = acc_t[head_rows:, :] + par_ref[0:1, :]
        sp_ref[...] = sp
        dt = jnp.maximum(sp, 0.0) + jnp.log1p(jnp.exp(-jnp.abs(sp)))
        dt_ref[...] = dt
        cum = triangle_sum(-par_ref[1:2, :] * dt, NN)
        cum_ref[...] = cum
        cumt_ref[...] = jnp.transpose(cum)[0:SLOT, :]
        last = cum[length - 1 :, :]
        write_weight = dt * jnp.exp(last - cum)
        read_weight = jnp.exp(cum)

        def conv(acc, taps, k):
            lo = k * LANES
            out = taps[0:1, lo : lo + LANES] * acc[start : start + length, lo : lo + LANES]
            for j in range(1, K):
                out += taps[j : j + 1, lo : lo + LANES] * acc[
                    start + j : start + j + length, lo : lo + LANES
                ]
            return out

        zb = conv(acc_s, cs_ref, 0)
        z_ref[:, inner : inner + LANES] = zb
        zc = conv(acc_s, cs_ref, 1)
        z_ref[:, inner + LANES :] = zc
        b2 = split(zb * sigmoid(zb))
        c2 = split(zc * sigmoid(zc))
        groups = N // 8
        pay_ref[:, 8 * tiles :, :] = jnp.zeros((2 * groups, 8, LANES), F32)
        for k in range(tiles):
            lo = k * LANES
            z = conv(acc_i, ci_ref, k)
            z_ref[:, lo : lo + LANES] = z
            x2 = split(z * sigmoid(z) * of_tile(write_weight, k))
            state = dot3(b2, x2, TN)
            g2 = split(cot_ref[:, lo : lo + LANES].astype(F32) * of_tile(read_weight, k))
            grad = dot3(c2, g2, TN)
            pay_ref[0:groups, 8 * k : 8 * k + 8, :] = state.reshape(groups, 8, LANES)
            pay_ref[groups:, 8 * k : 8 * k + 8, :] = grad.reshape(groups, 8, LANES)
            row = of_tile(last, k)
            pay_ref[:, 8 * tiles + k : 8 * tiles + k + 1, :] = jnp.broadcast_to(
                row[None], (2 * groups, 1, LANES)
            )


def ctx_scan_kernel(tiles, edge_ref, in_ref, out_ref):
    count = in_ref.shape[0]
    rows = 8 * tiles
    backward = edge_ref[0] >= count // 2

    def turn(i, held):
        at = jnp.where(backward, count - 1 - i, i)
        out_ref[at] = held
        got = in_ref[at]
        decay = jnp.exp(got[rows:, :])
        wide = jnp.concatenate(
            [jnp.broadcast_to(decay[k : k + 1, :], (8, LANES)) for k in range(tiles)], 0
        )
        return got[0:rows, :] + wide * held

    lax.fori_loop(0, count, turn, jnp.zeros((rows, LANES), F32), unroll=4)


def local_kernel(
    zv_ref, zb_ref, zc_ref, dt_ref, cum_ref, cumt_ref, cot_ref,
    y_ref, u_ref, db_ref, dc_ref,
    scores, grad_scores, dt_wide, cum_wide,
):
    tile = pl.program_id(0)
    length = zv_ref.shape[0]
    half = length // 2
    zb = zb_ref[...]
    zc = zc_ref[...]
    b = zb * sigmoid(zb)
    c = zc * sigmoid(zc)
    bh, bl = split(b)
    ch, cl = split(c)

    @pl.when(tile == 0)
    def _():
        row = lax.broadcasted_iota(jnp.int32, (half, half), 0)
        col = lax.broadcasted_iota(jnp.int32, (half, half), 1)
        for chunk in range(2):
            at = slice(chunk * half, (chunk + 1) * half)
            full = dot3((ch[at], cl[at]), (bh[at], bl[at]), NT)
            scores[chunk] = jnp.where(row >= col, full, 0.0)
        grad_scores[...] = jnp.zeros_like(grad_scores)
        db_ref[...] = jnp.zeros_like(db_ref)
        dc_ref[...] = jnp.zeros_like(dc_ref)

    lane = lax.broadcasted_iota(jnp.int32, (length, LANES), 1)

    def pick(ref):
        cols = ref[...]
        left = jnp.sum(jnp.where(lane == 2 * tile, cols, 0.0), 1, keepdims=True)
        right = jnp.sum(jnp.where(lane == 2 * tile + 1, cols, 0.0), 1, keepdims=True)
        return left, right

    dt_cols = pick(dt_ref)
    cum_cols = pick(cum_ref)
    dt_wide[...] = jnp.where(lane < P_SIZE, dt_cols[0], dt_cols[1])
    cum_wide[...] = jnp.where(lane < P_SIZE, cum_cols[0], cum_cols[1])
    zv = zv_ref[...]
    x = zv * sigmoid(zv) * dt_wide[...]
    g = cot_ref[...]
    xh, xl = split(x)
    gt = jnp.transpose(g.astype(F32)).astype(BF16)

    for chunk in range(2):
        at = slice(chunk * half, (chunk + 1) * half)
        ys = []
        us = []
        for head in range(2):
            of = slice(head * P_SIZE, (head + 1) * P_SIZE)
            row_logs = cumt_ref[pl.ds(2 * tile + head, 1), at]
            gaps = jnp.minimum(cum_cols[head][at] - row_logs, 0.0)
            decays = jnp.exp(gaps)
            weights = scores[chunk] * decays
            wh, wl = split(weights)
            x_pair = jnp.concatenate([xh[at, of], xl[at, of]], 1)
            y_pair = dot1(wh, x_pair, NN) + dot1(wl, x_pair, NN)
            ys.append(y_pair[:, 0:P_SIZE] + y_pair[:, P_SIZE:])
            us.append(dot1(gt[of, at], wh, NN) + dot1(gt[of, at], wl, NN))
            g_pair = jnp.concatenate([g[at, of], g[at, of]], 1)
            grad_scores[chunk] += dot1(g_pair, x_pair, NT) * decays
        y_ref[at, :] = jnp.concatenate(ys, 1)
        u_ref[at, :] = jnp.transpose(jnp.concatenate(us, 0))

    early = slice(0, half)
    late = slice(half, length)
    cum = cum_wide[...]
    middle = cum[half - 1 : half, :]
    down = jnp.exp(middle - cum[early])
    up = jnp.exp(cum[late] - middle)
    xd = split(x[early] * down)
    gd = split(g[late].astype(F32) * up)
    b0 = (bh[early], bl[early])
    c1 = (ch[late], cl[late])
    state = split(dot3(b0, xd, TN))
    grad = split(dot3(c1, gd, TN))
    y_ref[late, :] += up * dot3(c1, state, NN)
    u_ref[early, :] += down * dot3(b0, grad, NN)
    dc_ref[late, :] += dot3(gd, state, NT)
    db_ref[early, :] += dot3(xd, grad, NT)

    @pl.when(tile == pl.num_programs(0) - 1)
    def _():
        row = lax.broadcasted_iota(jnp.int32, (half, half), 0)
        col = lax.broadcasted_iota(jnp.int32, (half, half), 1)
        for chunk in range(2):
            at = slice(chunk * half, (chunk + 1) * half)
            gs = split(jnp.where(row >= col, grad_scores[chunk], 0.0))
            dc_ref[at, :] += dot3(gs, (bh[at], bl[at]), NN)
            db_ref[at, :] += dot3(gs, (ch[at], cl[at]), TN)


def join_kernel(
    tiles,
    z_ref, sp_ref, dt_ref, cum_ref, par_ref, cot_ref, y_ref, u_ref, db_ref, dc_ref,
    pay_ref, arrived_ref,
    mixed_ref, dconv_ref, gstep_ref,
):
    length = z_ref.shape[0]
    inner = tiles * LANES
    groups = N // 8
    dt = dt_ref[...]
    cum = cum_ref[...]
    last = cum[length - 1 :, :]
    read_weight = jnp.exp(cum)
    tail_weight = jnp.exp(last - cum)
    total_decay = jnp.exp(last)
    zb = z_ref[:, inner : inner + LANES]
    zc = z_ref[:, inner + LANES :]
    sb = sigmoid(zb)
    sc = sigmoid(zc)
    b2 = split(zb * sb)
    c2 = split(zc * sc)
    db = db_ref[...]
    dc = dc_ref[...]
    reads = jnp.zeros((length, LANES), F32)
    writes = jnp.zeros((length, LANES), F32)
    ends = jnp.zeros((1, LANES), F32)
    lane = lax.broadcasted_iota(jnp.int32, (LANES, LANES), 1)
    row = lax.broadcasted_iota(jnp.int32, (LANES, LANES), 0)
    for k in range(tiles):
        at = slice(k * LANES, (k + 1) * LANES)
        rows = slice(8 * k, 8 * k + 8)
        gather = jnp.where(lane == 2 * k + row // P_SIZE, 1.0, 0.0).astype(BF16)
        state = arrived_ref[0:groups, rows, :].reshape(N, LANES)
        grad = arrived_ref[groups:, rows, :].reshape(N, LANES)
        state2 = split(state)
        grad2 = split(grad)
        z = z_ref[:, at]
        s = sigmoid(z)
        v = z * s
        g = cot_ref[:, at].astype(F32)
        read_k = of_tile(read_weight, k)
        tail_k = of_tile(tail_weight, k)
        dt_k = of_tile(dt, k)
        skip = of_tile(par_ref[2:3, :], k)
        y = y_ref[:, at] + read_k * dot3(c2, state2, NN)
        u = u_ref[:, at] + tail_k * dot3(b2, grad2, NN)
        mixed_ref[:, at] = (y + skip * v).astype(BF16)
        dv = dt_k * u + skip * g
        dconv_ref[:, at] = dv * (s * (1.0 + z * (1.0 - s)))
        reads += dot2(split(g * y), gather, NN)
        writes += dot2(split(v * u), gather, NN)
        dc += dot3(split(g * read_k), state2, NT)
        db += dot3(split(v * dt_k * tail_k), grad2, NT)
        own = pay_ref[0:groups, rows, :].reshape(N, LANES)
        end = jnp.sum(grad * (own + of_tile(total_decay, k) * state), 0, keepdims=True)
        end = jnp.broadcast_to(end, (8, LANES))
        ends += dot2(split(end), gather, NN)[0:1]
    dconv_ref[:, inner : inner + LANES] = db * (sb * (1.0 + zb * (1.0 - sb)))
    dconv_ref[:, inner + LANES :] = dc * (sc * (1.0 + zc * (1.0 - sc)))
    grad_logs = triangle_sum(reads - dt * writes, TN) + ends
    grad_dt = writes - par_ref[1:2, :] * grad_logs
    gstep_ref[...] = grad_dt * sigmoid(sp_ref[...])


def conv_back_kernel(edge_ref, dconv_ref, rim_ref, ci_ref, cs_ref, gi_ref, gs_ref, gst_ref, wide):
    length = dconv_ref.shape[0]
    inner = ci_ref.shape[1]
    wide[0:length, :] = dconv_ref[...]
    wide[length:, :] = rim_ref[...] * jnp.where(edge_ref[1] == 0, 1.0, 0.0)

    def back(taps, offset, k):
        lo = k * LANES
        at = slice(offset + lo, offset + lo + LANES)
        out = taps[K - 1 : K, lo : lo + LANES] * wide[0:length, at]
        for j in range(1, K):
            out += taps[K - 1 - j : K - j, lo : lo + LANES] * wide[j : j + length, at]
        return out

    for k in range(inner // LANES):
        gi_ref[:, k * LANES : (k + 1) * LANES] = back(ci_ref, 0, k).astype(BF16)
    for k in range(2):
        at = slice(k * LANES, (k + 1) * LANES)
        grad = back(cs_ref, inner, k)
        gs_ref[:, at] = grad
        gst_ref[at, :] = jnp.transpose(grad)


def token_grad_kernel(heads, wi_ref, ws_ref, wt_ref, gi_ref, gs_ref, gstep_ref, out_ref, halves):
    shared = ws_ref.shape[1]

    @pl.when(pl.program_id(0) == 0)
    def _():
        high, low = split(gs_ref[...])
        halves[:, 0:shared] = high
        halves[:, shared : 2 * shared] = low
        high, low = split(gstep_ref[...])
        halves[:, 2 * shared : 2 * shared + LANES] = high
        halves[:, 2 * shared + LANES :] = low

    total = dot1(wi_ref[...], gi_ref[...], NT)
    total += dot1(ws_ref[...], halves[:, 0:shared], NT)
    total += dot1(ws_ref[...], halves[:, shared : 2 * shared], NT)
    wt = wt_ref[...]
    total += dot1(wt, halves[:, 2 * shared : 2 * shared + heads], NT)
    total += dot1(wt, halves[:, 2 * shared + LANES : 2 * shared + LANES + heads], NT)
    out_ref[0] = total


def weight_grad_kernel(tok_ref, gi_ref, out_ref):
    out_ref[...] = dot1(tok_ref[...], gi_ref[...], TN).reshape(out_ref.shape)


def side_grad_kernel(parts_ref, gstep_ref, tok_ref, out_ref, left):
    rows = parts_ref.shape[1]

    @pl.when(pl.program_id(0) == 0)
    def _():
        total = parts_ref[0]
        for i in range(1, parts_ref.shape[0]):
            total += parts_ref[i]
        steps = jnp.transpose(gstep_ref[...])[0:SLOT, :]
        high, low = split(jnp.concatenate([total, steps], 0))
        left[0] = high
        left[1] = low

    out_ref[...] = dot2((left[0], left[1]), tok_ref[...], NN)


def sum_kernel(parts_ref, out_ref):
    total = parts_ref[0]
    for i in range(1, parts_ref.shape[0]):
        total += parts_ref[i]
    out_ref[...] = jnp.transpose(total).astype(out_ref.dtype)


def whole(shape):
    return pl.BlockSpec(shape, lambda *_: (0,) * len(shape))


def smem():
    return pl.BlockSpec(memory_space=pltpu.SMEM)


def body(
    tokens,
    inner_weight,
    shared_weight,
    step_weight,
    conv_inner,
    conv_shared,
    step_bias,
    decay_rate,
    skip_gain,
    cotangent,
):
    length, width = tokens.shape
    inner = inner_weight.shape[1]
    shared = shared_weight.shape[1]
    heads = step_weight.shape[1]
    tiles = inner // LANES
    ctx = lax.axis_size("ctx")
    tp = lax.axis_size("tp")
    place = lax.axis_index("ctx")
    edge = jnp.stack([place, (place == ctx - 1).astype(jnp.int32)]).astype(jnp.int32)
    sds = jax.ShapeDtypeStruct

    rim = shifted(tokens[length - 8 :].astype(F32), "ctx", 1)
    params = jnp.pad(
        jnp.stack([step_bias, decay_rate, skip_gain]), ((0, 5), (0, LANES - heads))
    )

    block = 512
    total = inner + shared
    pay_rows = 8 * tiles + 8
    z, sp, dt, cum, cum_t, pay = pl.pallas_call(
        functools.partial(project_kernel, tiles, heads),
        grid=(width // block,),
        in_specs=[
            smem(),
            pl.BlockSpec((length, block), lambda i: (0, i)),
            pl.BlockSpec((8, block), lambda i: (0, i)),
            pl.BlockSpec((block, inner), lambda i: (i, 0)),
            pl.BlockSpec((block, shared), lambda i: (i, 0)),
            pl.BlockSpec((block, heads), lambda i: (i, 0)),
            whole((K, inner)),
            whole((K, shared)),
            whole((8, LANES)),
            whole((length, inner)),
        ],
        out_specs=[
            whole((length, total)),
            whole((length, LANES)),
            whole((length, LANES)),
            whole((length, LANES)),
            whole((SLOT, length)),
            whole((ctx, pay_rows, LANES)),
        ],
        out_shape=[
            sds((length, total), F32),
            sds((length, LANES), F32),
            sds((length, LANES), F32),
            sds((length, LANES), F32),
            sds((SLOT, length), F32),
            sds((ctx, pay_rows, LANES), F32),
        ],
        scratch_shapes=[
            pltpu.VMEM((length + 16, block), BF16),
            pltpu.VMEM((length + 16, inner), F32),
            pltpu.VMEM((length + 16, shared), F32),
            pltpu.VMEM((length + 16, LANES), F32),
        ],
        compiler_params=PARAMS,
        name="project",
    )(
        edge, tokens, rim, inner_weight, shared_weight, step_weight,
        conv_inner, conv_shared, params, cotangent,
    )

    by_rows = lax.all_to_all(pay, "ctx", 0, 0, tiled=True)

    y, u, db, dc = pl.pallas_call(
        local_kernel,
        grid=(tiles,),
        in_specs=[
            pl.BlockSpec((length, LANES), lambda i: (0, i)),
            pl.BlockSpec((length, LANES), lambda i: (0, tiles)),
            pl.BlockSpec((length, LANES), lambda i: (0, tiles + 1)),
            whole((length, LANES)),
            whole((length, LANES)),
            whole((SLOT, length)),
            pl.BlockSpec((length, LANES), lambda i: (0, i)),
        ],
        out_specs=[
            pl.BlockSpec((length, LANES), lambda i: (0, i)),
            pl.BlockSpec((length, LANES), lambda i: (0, i)),
            whole((length, LANES)),
            whole((length, LANES)),
        ],
        out_shape=[
            sds((length, inner), F32),
            sds((length, inner), F32),
            sds((length, LANES), F32),
            sds((length, LANES), F32),
        ],
        scratch_shapes=[
            pltpu.VMEM((2, length // 2, length // 2), F32),
            pltpu.VMEM((2, length // 2, length // 2), F32),
            pltpu.VMEM((length, LANES), F32),
            pltpu.VMEM((length, LANES), F32),
        ],
        compiler_params=PARAMS,
        cost_estimate=pl.CostEstimate(
            flops=10 * length * length * inner, bytes_accessed=8_000_000, transcendentals=0
        ),
        name="local",
    )(z, z, z, dt, cum, cum_t, cotangent)

    scanned = pl.pallas_call(
        functools.partial(ctx_scan_kernel, tiles),
        in_specs=[smem(), whole((ctx, pay_rows, LANES))],
        out_specs=whole((ctx, 8 * tiles, LANES)),
        out_shape=sds((ctx, 8 * tiles, LANES), F32),
        compiler_params=PARAMS,
        name="ctx_scan",
    )(edge, by_rows)
    arrived = lax.all_to_all(scanned, "ctx", 0, 0, tiled=True)

    mixed, dconv, gstep = pl.pallas_call(
        functools.partial(join_kernel, tiles),
        out_shape=[
            sds((length, inner), BF16),
            sds((length, total), F32),
            sds((length, LANES), F32),
        ],
        compiler_params=PARAMS,
        name="join",
    )(z, sp, dt, cum, params, cotangent, y, u, db, dc, pay, arrived)

    rim_back = shifted(dconv[0:8], "ctx", -1)
    grad_inner, grad_shared, grad_shared_t = pl.pallas_call(
        conv_back_kernel,
        in_specs=[
            smem(),
            whole((length, total)),
            whole((8, total)),
            whole((K, inner)),
            whole((K, shared)),
        ],
        out_specs=[whole((length, inner)), whole((length, shared)), whole((shared, length))],
        out_shape=[
            sds((length, inner), BF16),
            sds((length, shared), F32),
            sds((shared, length), F32),
        ],
        scratch_shapes=[pltpu.VMEM((length + 8, total), F32)],
        compiler_params=PARAMS,
        name="conv_back",
    )(edge, dconv, rim_back, conv_inner, conv_shared)

    shared_cols = shared // tp
    shared_parts = lax.all_to_all(
        grad_shared_t.reshape(tp, shared_cols, length), "tp", 0, 0, tiled=True
    )

    rows = width // ctx
    per = 8
    weight_parts = pl.pallas_call(
        weight_grad_kernel,
        grid=(ctx // per,),
        in_specs=[
            pl.BlockSpec((length, per * rows), lambda i: (0, i)),
            whole((length, inner)),
        ],
        out_specs=pl.BlockSpec((per, rows, inner), lambda i: (i, 0, 0)),
        out_shape=sds((ctx, rows, inner), F32),
        compiler_params=PARAMS,
        name="weight_grad",
    )(tokens, grad_inner)
    grad_inner_weight = lax.psum_scatter(weight_parts, "ctx", scatter_dimension=0, tiled=False)

    cols = width // tp
    token_parts = pl.pallas_call(
        functools.partial(token_grad_kernel, heads),
        grid=(tp,),
        in_specs=[
            pl.BlockSpec((cols, inner), lambda i: (i, 0)),
            pl.BlockSpec((cols, shared), lambda i: (i, 0)),
            pl.BlockSpec((cols, heads), lambda i: (i, 0)),
            whole((length, inner)),
            whole((length, shared)),
            whole((length, LANES)),
        ],
        out_specs=pl.BlockSpec((1, cols, length), lambda i: (i, 0, 0)),
        out_shape=sds((tp, cols, length), F32),
        scratch_shapes=[pltpu.VMEM((length, 2 * shared + 2 * LANES), BF16)],
        compiler_params=PARAMS,
        name="token_grad",
    )(inner_weight, shared_weight, step_weight, grad_inner, grad_shared, gstep)
    token_parts = lax.all_to_all(token_parts, "tp", 0, 0, tiled=True)

    side_rows = shared_cols + SLOT
    side = pl.pallas_call(
        side_grad_kernel,
        grid=(width // block,),
        in_specs=[
            whole((tp, shared_cols, length)),
            whole((length, LANES)),
            pl.BlockSpec((length, block), lambda i: (0, i)),
        ],
        out_specs=pl.BlockSpec((side_rows, block), lambda i: (0, i)),
        out_shape=sds((side_rows, width), F32),
        scratch_shapes=[pltpu.VMEM((2, side_rows, length), BF16)],
        compiler_params=PARAMS,
        name="side_grad",
    )(shared_parts, gstep, tokens)
    side = jnp.transpose(side.reshape(side_rows, ctx, rows), (1, 0, 2))
    side = jnp.sum(lax.all_to_all(side, "ctx", 0, 0, tiled=True), 0).T

    grad_tokens = pl.pallas_call(
        sum_kernel,
        out_shape=sds((length, cols), BF16),
        compiler_params=PARAMS,
        name="token_sum",
    )(token_parts)
    return (
        mixed,
        grad_tokens,
        grad_inner_weight,
        side[:, :shared_cols],
        side[:, shared_cols : shared_cols + heads],
    )


def solution(mesh):
    in_specs = (
        P("ctx", None),
        P(None, "tp"),
        P(),
        P(None, "tp"),
        P(None, "tp"),
        P(),
        P("tp"),
        P("tp"),
        P("tp"),
        P("ctx", "tp"),
    )
    out_specs = (P("ctx", "tp"), P("ctx", "tp"), P("ctx", "tp"), P("ctx", "tp"), P("ctx", "tp"))
    return jax.shard_map(body, mesh=mesh, in_specs=in_specs, out_specs=out_specs, check_vma=False)
```

time: 1500 us -> 282 us (0.19)
  waiting for transfers between devices: 744 us -> 105 us
  starting transfers between devices: 234 us -> 22.7 us
  other arithmetic: 196 us -> 2.79 us
  local copies, waits for them, and re-layouts: 186 us -> 32.7 us
  matrix products: 111 us -> 0 us
  Pallas kernels: 0 us -> 52.3 us
  blocking collectives: 0 us -> 49.8 us
    ppermute x64 -> x2, waiting for transfers between devices: 485 us -> 3.8 us  [shifted(): lax.ppermute(block, axis, [(i, (i + distance) % size) for i in range(size)])]
    ppermute x64 -> x2, starting transfers between devices: 234 us -> 4.78 us  [shifted(): lax.ppermute(block, axis, [(i, (i + distance) % size) for i in range(size)])]
    unnamed x5 -> x1, waiting for transfers between devices: 166 us -> 0.02 us
    add x65 -> x0, other arithmetic: 119 us -> none  [the longest x31 58.7 us: backward_combine(): later[1] + jnp.exp(later[0])[:, None, None] * earlier[1]]
    dot_general x36 -> x0, matrix products: 111 us -> none  [the longest x6 32.4 us: group_terms(): jnp.einsum('ijh,jhp->ihp', weights, values, precision=lax.Precision.HIGHEST)]
    all_to_all x0 -> x3, waiting for transfers between devices: none -> 91.1 us  [the longest x1 82.9 us: body(): token_parts = lax.all_to_all(token_parts, 'tp', 0, 0, tiled=True)]
    reduce_scatter x1, waiting for transfers between devices: 92.6 us -> 10.5 us  [body(): lax.psum_scatter(weight_parts, 'ctx', scatter_dimension=0, tiled=False)]
    dynamic_update_slice x22 -> x0, local copies, waits for them, and re-layouts: 77.7 us -> none  [local_mixer(): lax.scan(advance, start_carry, (values, b_vectors, c_vectors, step_size))]
  transfers between devices with their start and end apart: 67 -> 6, of which waited for: 65 -> 5; matrix products, arithmetic and copies ran while one was open for 4% -> 2% of each run, Pallas kernels for 0% -> 11%
where the time goes in v1:
time: 282 us; the launch traced here: 280 us
  waiting for transfers between devices  105 us (37%)
  Pallas kernels  52.3 us (19%)
  blocking collectives  49.8 us (18%)
  local copies, waits for them, and re-layouts  32.7 us (12%)
  starting transfers between devices  22.7 us (8%)
  between operations  14.2 us (5%)
    all_to_all x1, waiting for transfers between devices, body(): token_parts = lax.all_to_all(token_parts, 'tp', 0, 0, tiled=True)  82.9 us
    all_to_all x1, blocking collectives, body(): by_rows = lax.all_to_all(pay, 'ctx', 0, 0, tiled=True)  33.2 us
    unnamed x70, local copies, waits for them, and re-layouts  25.7 us
    all_to_all x1, blocking collectives, body(): lax.all_to_all(grad_shared_t.reshape(tp, shared_cols, length), 'tp', 0, 0...  16.5 us
    pallas_call x1, Pallas kernels, body(): pl.pallas_call(local_kernel, grid=(tiles,), in_specs=[pl.BlockSpec((lengt...  12.1 us
    pallas_call x1, Pallas kernels, body(): pl.pallas_call(functools.partial(project_kernel, tiles, heads), grid=(wid...  10.9 us
    reduce_scatter x1, waiting for transfers between devices, body(): lax.psum_scatter(weight_parts, 'ctx', scatter_dimension=0, tiled=False)  10.5 us
    pallas_call x1, Pallas kernels, body(): pl.pallas_call(functools.partial(token_grad_kernel, heads), grid=(tp,), i...  9.82 us
  transfers between devices with their start and end apart: 6, of which 5 were waited for; matrix products, arithmetic and copies ran while one was open for 2% of the time, Pallas kernels for 11%

profile of v1, /device:TPU:1, one launch (start us, length us, event | category | flops | bytes accessed | tf_op | source)
XLA Modules:
  0.0 279.9 jit_solution(16308906010292374683)
XLA Ops:
  7.2 0.8 slice_convert_fusion
  8.0 4.4 %collective-permute-start = (f32[8,2560]{1,0:T(8,128)S(1)}, f32[8,2560]{1,0:T(8,128)S(1)}, u32[]{:S(2)}, u32[]{:S(2)}) collective-permute-start(f32[8,2560]{1,0:T(8,128)S(1)} %slice_convert_fusion), channel_id=1, source_target_pairs={{0,8},{8,16},{16,24},{24,32},{32,40},{40,48},{48,56},{56,64},{64,7... | collective-permute-start | bytes 245768 | tf_op jit(solution)/shard_map/ppermute | solution.py:25
  12.3 1.2 copy.18.wt_ref
  14.4 1.1 copy-done.2
  15.4 1.3 copy-done.4
  16.8 0.7 copy-done.30
  18.2 10.9 %project.1 = (f32[512,896]{1,0:T(8,128)S(1)}, f32[512,128]{1,0:T(8,128)S(1)}, f32[512,128]{1,0:T(8,128)S(1)}, f32[512,128]{1,0:T(8,128)S(1)}, f32[16,512]{1,0:T(8,128)S(1)}, /*index=5*/f32[32,48,128]{2,1,0:T(8,128)S(1)}) custom-call(s32[2]{0:T(128)S(1)} %pad_add_fusion.edge_ref, bf16[512,2560]{1,0:T(8,128)(2,1)} %tok_ref.5, ...), custom_call_target="tpu_custom_call" | custom-call | tf_op jit(solution)/shard_map/project/pallas_call | solution.py:432
  29.1 0.7 copy-done.17
  29.8 0.7 copy-done.24
  30.5 33.2 %all_to_all.25.in_ref = f32[32,48,128]{2,1,0:T(8,128)S(1)} all-to-all(f32[32,48,128]{2,1,0:T(8,128)S(1)} %get-tuple-element.30.pay_ref), channel_id=1, replica_groups=mesh['ctx'=32,'tp'=8] {'ctx'}, dimensions={0} | all-to-all | bytes 1572864 | tf_op jit(solution)/shard_map/all_to_all | solution.py:476
  63.7 0.9 copy-done.6
  65.3 0.8 copy-done.11
  66.1 6.9 %all-to-all-start.1 = ((f32[32,40,128]{2,1,0:T(8,128)}), f32[32,40,128]{2,1,0:T(8,128)}, u32[]{:S(2)}, u32[]{:S(2)}) async-start(f32[32,40,128]{2,1,0:T(8,128)} %copy-done.11), calls=%async_computation.1 | async-start | bytes 1310720 | tf_op jit(solution)/shard_map/all_to_all | solution.py:523
  73.0 0.9 copy-done.18
  74.0 12.1 %local.1 = (f32[512,640]{1,0:T(8,128)S(1)}, f32[512,640]{1,0:T(8,128)S(1)}, f32[512,128]{1,0:T(8,128)S(1)}, f32[512,128]{1,0:T(8,128)S(1)}) custom-call(f32[512,896]{1,0:T(8,128)S(1)} %get-tuple-element.21.zv_ref.zb_ref.zc_ref.z_ref, f32[512,896]{1,0:T(8,128)S(1)} %get-tuple-element.21.zv_ref.zb_ref.zc_ref.z_ref, ...), custom_call_target="tpu_custom_call" | custom-call | flops 1677721600 | bytes 8000000 | tf_op jit(solution)/shard_map/local/pallas_call | solution.py:478
  86.1 1.1 copy-done.14
  87.2 1.1 copy-done.16
  89.0 0.7 copy-done.28
  89.7 2.3 all-to-all-done.1.arrived_ref
  92.0 1.1 copy-done.7
  93.1 1.3 copy-done.15
  94.5 0.9 copy-done.19
  95.4 0.9 copy-done.25
  96.4 0.9 copy-done.27
  97.3 0.9 copy-done.29
  98.3 7.8 %join.1 = (bf16[512,640]{1,0:T(8,128)(2,1)}, f32[512,896]{1,0:T(8,128)}, f32[512,128]{1,0:T(8,128)S(1)}) custom-call(f32[512,896]{1,0:T(8,128)} %copy-done, f32[512,128]{1,0:T(8,128)S(1)} %copy-done.25, f32[512,128]{1,0:T(8,128)S(1)} %get-tuple-element.23.dt_ref, f32[512,128]{1,0:T(8,128)S(1)} %copy-done.19, f32[8,128]{1,0:T(8,128)S(1)} %select_maximum_fusion.par_ref, ...), custom_call_target="tpu_custom_call" | custom-call | tf_op jit(solution)/shard_map/join/pallas_call | solution.py:525
  106.0 0.9 slice.13
  107.3 3.8 %collective-permute-done.1.rim_ref = f32[8,896]{1,0:T(8,128)S(1)} collective-permute-done((f32[8,896]{1,0:T(8,128)S(1)}, f32[8,896]{1,0:T(8,128)S(1)}, u32[]{:S(2)}, u32[]{:S(2)}) %collective-permute-start.1) | collective-permute-done | bytes 28704 | tf_op jit(solution)/shard_map/ppermute | solution.py:25
  111.1 1.5 copy-done.13
  112.6 1.6 conv_back.1
  114.3 0.8 copy-done.8
  115.1 16.5 %all_to_all.26.parts_ref = f32[8,32,512]{2,1,0:T(8,128)S(1)} all-to-all(f32[8,32,512]{2,1,0:T(8,128)S(1)} %bitcast.11), channel_id=1, replica_groups=mesh['ctx'=32,'tp'=8] {'tp'}, dimensions={0} | all-to-all | bytes 1048576 | tf_op jit(solution)/shard_map/all_to_all | solution.py:558
  131.7 1.9 side_grad.1
  133.6 0.8 copy-done.12
  134.3 2.3 reshape.17
  136.7 2.5 copy.23
  139.2 6.3 %all-to-all-start.4 = ((f32[32,48,80]{2,1,0:T(8,128)}), f32[32,48,80]{2,1,0:T(8,128)}, u32[]{:S(2)}, u32[]{:S(2)}) async-start(f32[32,48,80]{2,1,0:T(8,128)} %bitcast.12), calls=%async_computation.5 | async-start | bytes 1572864 | tf_op jit(solution)/shard_map/all_to_all | solution.py:614
  145.6 1.1 copy-done.9
  146.6 4.8 %weight_grad.1 = f32[32,80,640]{2,1,0:T(8,128)} custom-call(bf16[512,2560]{1,0:T(8,128)(2,1)S(1)} %copy-done.1, bf16[512,640]{1,0:T(8,128)(2,1)S(1)} %copy-done.9), custom_call_target="tpu_custom_call" | custom-call | tf_op jit(solution)/shard_map/weight_grad/pallas_call | solution.py:564
  151.4 1.3 copy-done.5
  153.1 9.8 %token_grad.1 = f32[8,320,512]{2,1,0:T(8,128)} custom-call(bf16[2560,640]{1,0:T(8,128)(2,1)} %wi_ref.3, bf16[2560,256]{1,0:T(8,128)(2,1)S(1)} %copy-done.5, bf16[2560,10]{1,0:T(8,128)(2,1)S(1)} %copy.18.wt_ref, bf16[512,640]{1,0:T(8,128)(2,1)S(1)} %copy-done.10, f32[512,256]{1,0:T(8,128)S(1)} %copy-done.23, f32[512,128]{1,0:T(8,128)S(1)} %copy-done.21), custom_call_target="tpu_custom_call" | custom-call | tf_op jit(solution)/shard_map/token_grad/pallas_call | solution.py:579
  162.9 5.9 %all-to-all-done.4 = f32[32,48,80]{2,1,0:T(8,128)} async-done(((f32[32,48,80]{2,1,0:T(8,128)}), f32[32,48,80]{2,1,0:T(8,128)}, u32[]{:S(2)}, u32[]{:S(2)}) %all-to-all-start.4) | async-done | bytes 491552 | tf_op jit(solution)/shard_map/all_to_all | solution.py:614
  168.8 4.7 %all-to-all-start.2 = ((f32[8,320,512]{2,1,0:T(8,128)}), f32[8,320,512]{2,1,0:T(8,128)}, u32[]{:S(2)}, u32[]{:S(2)}) async-start(f32[8,320,512]{2,1,0:T(8,128)} %token_grad.1), calls=%async_computation.2 | async-start | bytes 10485760 | tf_op jit(solution)/shard_map/all_to_all | solution.py:596
  173.5 1.2 reduce_sum.9
  175.9 82.9 %all-to-all-done.2.parts_ref = f32[8,320,512]{2,1,0:T(8,128)} async-done(((f32[8,320,512]{2,1,0:T(8,128)}), f32[8,320,512]{2,1,0:T(8,128)}, u32[]{:S(2)}, u32[]{:S(2)}) %all-to-all-start.2) | async-done | bytes 5242912 | tf_op jit(solution)/shard_map/all_to_all | solution.py:596
  258.9 2.8 %token_sum.1 = bf16[512,320]{1,0:T(8,128)(2,1)S(1)} custom-call(f32[8,320,512]{2,1,0:T(8,128)} %all-to-all-done.2.parts_ref), custom_call_target="tpu_custom_call" | custom-call | tf_op jit(solution)/shard_map/token_sum/pallas_call | solution.py:616
  261.7 0.9 copy.21
  262.6 10.5 %reduce-scatter.2.cloned.1.call-done = f32[1,80,640]{2,1,0:T(8,128)} async-done(((f32[32,80,640]{2,1,0:T(8,128)}), f32[1,80,640]{2,1,0:T(8,128)}) %reduce-scatter.2.cloned.1.call-update) | async-done | bytes 204816 | tf_op jit(solution)/shard_map/reduce_scatter | solution.py:576
  (55 shorter events, 5.0 us)
Async XLA Ops:
  8.0 6.4 %collective-permute-start = (f32[8,2560]{1,0:T(8,128)S(1)}, f32[8,2560]{1,0:T(8,128)S(1)}, u32[]{:S(2)}, u32[]{:S(2)}) collective-permute-start(f32[8,2560]{1,0:T(8,128)S(1)} %slice_convert_fusion), channel_id=1, source_target_pairs={{0,8},{8,16},{16,24},{24,32},{32,40},{40,48},{48,56},{56,64},{64,7... | collective-permute-start | bytes 245768 | tf_op jit(solution)/shard_map/ppermute | solution.py:25
  14.4 1.1 copy-start.2
  15.4 1.3 copy-start.4
  16.8 0.7 copy-start.30
  17.5 0.7 copy-start.32
  29.0 0.7 copy-start.17
  29.8 0.7 copy-start.24
  30.5 55.7 %copy-start = (f32[512,896]{1,0:T(8,128)}, f32[512,896]{1,0:T(8,128)S(1)}, u32[]{:S(2)}) copy-start(f32[512,896]{1,0:T(8,128)S(1)} %get-tuple-element.21.zv_ref.zb_ref.zc_ref.z_ref) | copy-start | bytes 5505028
  30.5 42.6 %copy-start.3 = (bf16[512,640]{1,0:T(8,128)(2,1)S(1)}, bf16[512,640]{1,0:T(8,128)(2,1)}, u32[]{:S(2)}) copy-start(bf16[512,640]{1,0:T(8,128)(2,1)} %cot_ref.5) | copy-start | bytes 1966084
  63.7 0.9 copy-start.6
  65.3 0.8 copy-start.11
  66.1 25.9 %all-to-all-start.1 = ((f32[32,40,128]{2,1,0:T(8,128)}), f32[32,40,128]{2,1,0:T(8,128)}, u32[]{:S(2)}, u32[]{:S(2)}) async-start(f32[32,40,128]{2,1,0:T(8,128)} %copy-done.11), calls=%async_computation.1 | async-start | bytes 1310720 | tf_op jit(solution)/shard_map/all_to_all | solution.py:523
  73.0 1.0 copy-start.18
  86.1 1.1 copy-start.14
  87.2 1.1 copy-start.16
  88.3 0.7 copy-start.26
  89.0 0.7 copy-start.28
  92.0 1.1 copy-start.7
  93.1 1.3 copy-start.15
  94.4 0.9 copy-start.19
  95.4 0.9 copy-start.25
  96.4 0.9 copy-start.27
  97.3 0.9 copy-start.29
  98.3 12.9 %copy-start.31 = (f32[4,640]{1,0:T(4,128)S(1)}, f32[4,640]{1,0:T(4,128)}, u32[]{:S(2)}) copy-start(f32[4,640]{1,0:T(4,128)} %ci_ref.3) | copy-start | bytes 30724
  98.3 12.9 %copy-start.33 = (f32[4,256]{1,0:T(4,128)S(1)}, f32[4,256]{1,0:T(4,128)}, u32[]{:S(2)}) copy-start(f32[4,256]{1,0:T(4,128)} %cs_ref.3) | copy-start | bytes 12292
  106.0 25.7 %copy-start.20 = (f32[512,128]{1,0:T(8,128)}, f32[512,128]{1,0:T(8,128)S(1)}, u32[]{:S(2)}) copy-start(f32[512,128]{1,0:T(8,128)S(1)} %get-tuple-element.35.gstep_ref) | copy-start | bytes 786436
  106.0 25.7 %copy-start.1 = (bf16[512,2560]{1,0:T(8,128)(2,1)S(1)}, bf16[512,2560]{1,0:T(8,128)(2,1)}, u32[]{:S(2)}) copy-start(bf16[512,2560]{1,0:T(8,128)(2,1)} %tok_ref.5) | copy-start | bytes 7864324
  106.9 4.2 %collective-permute-start.1 = (f32[8,896]{1,0:T(8,128)S(1)}, f32[8,896]{1,0:T(8,128)S(1)}, u32[]{:S(2)}, u32[]{:S(2)}) collective-permute-start(f32[8,896]{1,0:T(8,128)S(1)} %slice.13), channel_id=1, source_target_pairs={{0,248},{8,0},{16,8},{24,16},{32,24},{40,32},{48,40},{56,48},{64,5... | collective-permute-start | bytes 86024 | tf_op jit(solution)/shard_map/ppermute | solution.py:25
  111.1 1.5 copy-start.13
  114.3 0.8 copy-start.8
  115.1 16.5 %copy-start.22 = (f32[512,256]{1,0:T(8,128)}, f32[512,256]{1,0:T(8,128)S(1)}, u32[]{:S(2)}) copy-start(f32[512,256]{1,0:T(8,128)S(1)} %get-tuple-element.34.gs_ref) | copy-start | bytes 1572868
  133.5 0.8 copy-start.12
  139.2 29.6 %all-to-all-start.4 = ((f32[32,48,80]{2,1,0:T(8,128)}), f32[32,48,80]{2,1,0:T(8,128)}, u32[]{:S(2)}, u32[]{:S(2)}) async-start(f32[32,48,80]{2,1,0:T(8,128)} %bitcast.12), calls=%async_computation.5 | async-start | bytes 1572864 | tf_op jit(solution)/shard_map/all_to_all | solution.py:614
  145.5 127.5 %reduce-scatter.2.cloned.1.call-start = ((), (), s32[]{:S(2)}) async-start(), calls=%async_computation.6 | async-start | bytes 6758400 | tf_op jit(solution)/shard_map/reduce_scatter | solution.py:576
  145.6 1.1 copy-start.9
  151.4 1.3 copy-start.5
  151.4 1.5 copy-start.10
  151.4 1.5 copy-start.21
  151.4 1.7 copy-start.23
  168.8 90.1 %all-to-all-start.2 = ((f32[8,320,512]{2,1,0:T(8,128)}), f32[8,320,512]{2,1,0:T(8,128)}, u32[]{:S(2)}, u32[]{:S(2)}) async-start(f32[8,320,512]{2,1,0:T(8,128)} %token_grad.1), calls=%async_computation.2 | async-start | bytes 10485760 | tf_op jit(solution)/shard_map/all_to_all | solution.py:596
Sparse Core Ops, SparseCore 0:
  151.6 121.4 reduce-scatter.1

commit v2 on v1

v2 whole, which is shorter than its diff:
```python
import functools

import jax
import jax.numpy as jnp
from jax import lax
from jax.experimental import pallas as pl
from jax.experimental.pallas import tpu as pltpu
from jax.sharding import PartitionSpec as P

P_SIZE = 64
N = 128
K = 4
LANES = 128
SLOT = 16
CORES = 2
RING = 4
F32 = jnp.float32
BF16 = jnp.bfloat16
NN = (((1,), (0,)), ((), ()))
NT = (((1,), (1,)), ((), ()))
TN = (((0,), (0,)), ((), ()))
PARAMS = pltpu.CompilerParams(vmem_limit_bytes=60 * 1024 * 1024)


def shifted(block, axis, distance):
    size = lax.axis_size(axis)
    return lax.ppermute(block, axis, [(i, (i + distance) % size) for i in range(size)])


def ctx_shift(block, dy, dz, dcore):
    def at(y, z, core):
        return (y % RING) * RING * CORES + (z % RING) * CORES + core % CORES

    route = [
        (at(y, z, core), at(y + dy, z + dz, core + dcore))
        for y in range(RING)
        for z in range(RING)
        for core in range(CORES)
    ]
    return lax.ppermute(block, "ctx", route)


def dot1(a, b, dims):
    return lax.dot_general(a, b, dims, preferred_element_type=F32)


def split(a):
    high = a.astype(BF16)
    return high, (a - high.astype(F32)).astype(BF16)


def dot3(a, b, dims):
    ah, al = a
    bh, bl = b
    return dot1(ah, bh, dims) + (dot1(ah, bl, dims) + dot1(al, bh, dims))


def dot2(a, b, dims):
    return dot1(a[0], b, dims) + dot1(a[1], b, dims)


def sigmoid(z):
    return 1.0 / (1.0 + jnp.exp(-z))


def of_tile(cols, k):
    lane = lax.broadcasted_iota(jnp.int32, (cols.shape[0], LANES), 1)
    left = jnp.broadcast_to(cols[:, 2 * k : 2 * k + 1], lane.shape)
    right = jnp.broadcast_to(cols[:, 2 * k + 1 : 2 * k + 2], lane.shape)
    return jnp.where(lane < P_SIZE, left, right)


def moving_tile(cols, k):
    return of_tile(pltpu.roll(cols, (LANES - 2 * k) % LANES, 1), 0)


def triangle_sum(a, dims):
    length = a.shape[0]
    row = lax.broadcasted_iota(jnp.int32, (length, length), 0)
    col = lax.broadcasted_iota(jnp.int32, (length, length), 1)
    reach = row >= col if dims == NN else row <= col
    ones = jnp.where(reach, 1.0, 0.0).astype(BF16)
    first = a.astype(BF16).astype(F32)
    second = (a - first).astype(BF16).astype(F32)
    third = (a - first - second).astype(BF16).astype(F32)
    packed = first + pltpu.roll(second, SLOT, 1) + pltpu.roll(third, 2 * SLOT, 1)
    sums = dot1(ones, packed.astype(BF16), NN)
    total = sums + pltpu.roll(sums, LANES - SLOT, 1) + pltpu.roll(sums, LANES - 2 * SLOT, 1)
    lane = lax.broadcasted_iota(jnp.int32, total.shape, 1)
    return jnp.where(lane < SLOT, total, 0.0)


def project_kernel(
    tiles, heads,
    edge_ref, tok_ref, rim_ref, wi_ref, ws_ref, wt_ref, ci_ref, cs_ref, par_ref, cot_ref,
    z_ref, sp_ref, dt_ref, cum_ref, cumt_ref, keep_ref, send_ref,
    lhs, acc_i, acc_s, acc_t,
):
    step = pl.program_id(0)
    length = tok_ref.shape[0]
    head_rows = lhs.shape[0] - length
    inner = wi_ref.shape[1]

    @pl.when(step == 0)
    def _():
        acc_i[...] = jnp.zeros_like(acc_i)
        acc_s[...] = jnp.zeros_like(acc_s)
        acc_t[...] = jnp.zeros_like(acc_t)

    keep = jnp.where(edge_ref[0] == 0, 0.0, 1.0)
    rim = rim_ref[...] * keep
    lhs[0:head_rows, :] = jnp.concatenate([jnp.zeros_like(rim), rim], 0).astype(BF16)
    lhs[head_rows:, :] = tok_ref[...]
    left = lhs[...]
    acc_i[...] += dot1(left, wi_ref[...], NN)
    acc_s[...] += dot1(left, ws_ref[...], NN)
    acc_t[:, 0:heads] += dot1(left, wt_ref[...], NT)

    @pl.when(step == pl.num_programs(0) - 1)
    def _():
        start = head_rows - (K - 1)
        sp = acc_t[head_rows:, :] + par_ref[0:1, :]
        sp_ref[...] = sp
        dt = jnp.maximum(sp, 0.0) + jnp.log1p(jnp.exp(-jnp.abs(sp)))
        dt_ref[...] = dt
        cum = triangle_sum(-par_ref[1:2, :] * dt, NN)
        cum_ref[...] = cum
        cumt_ref[...] = jnp.transpose(cum)[0:SLOT, :]
        last = cum[length - 1 :, :]
        write_weight = dt * jnp.exp(last - cum)
        read_weight = jnp.exp(cum)

        def conv(acc, taps, k):
            lo = k * LANES
            out = taps[0:1, lo : lo + LANES] * acc[start : start + length, lo : lo + LANES]
            for j in range(1, K):
                out += taps[j : j + 1, lo : lo + LANES] * acc[
                    start + j : start + j + length, lo : lo + LANES
                ]
            return out

        zb = conv(acc_s, cs_ref, 0)
        z_ref[:, inner : inner + LANES] = zb
        zc = conv(acc_s, cs_ref, 1)
        z_ref[:, inner + LANES :] = zc
        b2 = split(zb * sigmoid(zb))
        c2 = split(zc * sigmoid(zc))
        groups = N // 8
        forward = edge_ref[2] == 0
        blank = jnp.zeros((groups, 8, LANES), F32)
        keep_ref[:, 8 * tiles :, :] = blank
        send_ref[:, 8 * tiles :, :] = blank
        for k in range(tiles):
            lo = k * LANES
            rows = slice(8 * k, 8 * k + 8)
            z = conv(acc_i, ci_ref, k)
            z_ref[:, lo : lo + LANES] = z
            x2 = split(z * sigmoid(z) * of_tile(write_weight, k))
            state = dot3(b2, x2, TN)
            g2 = split(cot_ref[:, lo : lo + LANES].astype(F32) * of_tile(read_weight, k))
            grad = dot3(c2, g2, TN)
            keep_ref[:, rows, :] = jnp.where(forward, state, grad).reshape(groups, 8, LANES)
            send_ref[:, rows, :] = jnp.where(forward, grad, state).reshape(groups, 8, LANES)
            row = jnp.broadcast_to(of_tile(last, k)[None], (groups, 1, LANES))
            keep_ref[:, 8 * tiles + k : 8 * tiles + k + 1, :] = row
            send_ref[:, 8 * tiles + k : 8 * tiles + k + 1, :] = row


def decay_rows(tiles, block):
    decay = jnp.exp(block[..., 8 * tiles :, :])
    shape = block.shape[:-2] + (8, LANES)
    return jnp.concatenate(
        [jnp.broadcast_to(decay[..., k : k + 1, :], shape) for k in range(tiles)], -2
    )


def chip_kernel(tiles, keep_ref, got_ref, out_ref):
    rows = 8 * tiles
    for i in range(keep_ref.shape[0]):
        keep = keep_ref[i]
        got = got_ref[i]
        out_ref[i, 0:rows, :] = got[0:rows, :] + decay_rows(tiles, got) * keep[0:rows, :]
        out_ref[i, rows:, :] = got[rows:, :] + keep[rows:, :]


def onward_kernel(tiles, keep_ref, arrived_ref, out_ref):
    rows = 8 * tiles
    for i in range(keep_ref.shape[0]):
        keep = keep_ref[i]
        out_ref[i] = keep[0:rows, :] + decay_rows(tiles, keep) * arrived_ref[i]


def ctx_scan_kernel(tiles, edge_ref, in_ref, after_ref, out_ref):
    count = in_ref.shape[0]
    rows = 8 * tiles
    backward = edge_ref[2] == 1

    def turn(i, held):
        at = jnp.where(backward, count - 1 - i, i)
        out_ref[at] = held
        got = in_ref[at]
        return got[0:rows, :] + decay_rows(tiles, got) * held

    lax.fori_loop(0, count, turn, jnp.zeros((rows, LANES), F32), unroll=4)


def local_kernel(
    zv_ref, zb_ref, zc_ref, dt_ref, cum_ref, cumt_ref, cot_ref,
    y_ref, u_ref, db_ref, dc_ref,
    scores, grad_scores, dt_wide, cum_wide,
):
    tile = pl.program_id(0)
    length = zv_ref.shape[0]
    half = length // 2
    zb = zb_ref[...]
    zc = zc_ref[...]
    b = zb * sigmoid(zb)
    c = zc * sigmoid(zc)
    bh, bl = split(b)
    ch, cl = split(c)

    @pl.when(tile == 0)
    def _():
        row = lax.broadcasted_iota(jnp.int32, (half, half), 0)
        col = lax.broadcasted_iota(jnp.int32, (half, half), 1)
        for chunk in range(2):
            at = slice(chunk * half, (chunk + 1) * half)
            full = dot3((ch[at], cl[at]), (bh[at], bl[at]), NT)
            scores[chunk] = jnp.where(row >= col, full, 0.0)
        grad_scores[...] = jnp.zeros_like(grad_scores)
        db_ref[...] = jnp.zeros_like(db_ref)
        dc_ref[...] = jnp.zeros_like(dc_ref)

    lane = lax.broadcasted_iota(jnp.int32, (length, LANES), 1)

    def pick(ref):
        cols = pltpu.roll(ref[...], (LANES - 2 * tile) % LANES, 1)
        return cols[:, 0:1], cols[:, 1:2]

    dt_cols = pick(dt_ref)
    cum_cols = pick(cum_ref)
    dt_wide[...] = jnp.where(lane < P_SIZE, dt_cols[0], dt_cols[1])
    cum_wide[...] = jnp.where(lane < P_SIZE, cum_cols[0], cum_cols[1])
    zv = zv_ref[...]
    x = zv * sigmoid(zv) * dt_wide[...]
    g = cot_ref[...]
    xh, xl = split(x)
    gt = jnp.transpose(g.astype(F32)).astype(BF16)

    for chunk in range(2):
        at = slice(chunk * half, (chunk + 1) * half)
        ys = []
        us = []
        for head in range(2):
            of = slice(head * P_SIZE, (head + 1) * P_SIZE)
            row_logs = cumt_ref[pl.ds(2 * tile + head, 1), at]
            gaps = jnp.minimum(cum_cols[head][at] - row_logs, 0.0)
            decays = jnp.exp(gaps)
            weights = scores[chunk] * decays
            wh, wl = split(weights)
            x_pair = jnp.concatenate([xh[at, of], xl[at, of]], 1)
            y_pair = dot1(wh, x_pair, NN) + dot1(wl, x_pair, NN)
            ys.append(y_pair[:, 0:P_SIZE] + y_pair[:, P_SIZE:])
            us.append(dot1(gt[of, at], wh, NN) + dot1(gt[of, at], wl, NN))
            g_pair = jnp.concatenate([g[at, of], g[at, of]], 1)
            grad_scores[chunk] += dot1(g_pair, x_pair, NT) * decays
        y_ref[at, :] = jnp.concatenate(ys, 1)
        u_ref[at, :] = jnp.transpose(jnp.concatenate(us, 0))

    early = slice(0, half)
    late = slice(half, length)
    cum = cum_wide[...]
    middle = cum[half - 1 : half, :]
    down = jnp.exp(middle - cum[early])
    up = jnp.exp(cum[late] - middle)
    xd = split(x[early] * down)
    gd = split(g[late].astype(F32) * up)
    b0 = (bh[early], bl[early])
    c1 = (ch[late], cl[late])
    state = split(dot3(b0, xd, TN))
    grad = split(dot3(c1, gd, TN))
    y_ref[late, :] += up * dot3(c1, state, NN)
    u_ref[early, :] += down * dot3(b0, grad, NN)
    dc_ref[late, :] += dot3(gd, state, NT)
    db_ref[early, :] += dot3(xd, grad, NT)

    @pl.when(tile == pl.num_programs(0) - 1)
    def _():
        row = lax.broadcasted_iota(jnp.int32, (half, half), 0)
        col = lax.broadcasted_iota(jnp.int32, (half, half), 1)
        for chunk in range(2):
            at = slice(chunk * half, (chunk + 1) * half)
            gs = split(jnp.where(row >= col, grad_scores[chunk], 0.0))
            dc_ref[at, :] += dot3(gs, (bh[at], bl[at]), NN)
            db_ref[at, :] += dot3(gs, (ch[at], cl[at]), TN)


def join_kernel(
    tiles,
    edge_ref, zv_ref, zb_ref, zc_ref, sp_ref, dt_ref, cum_ref, par_ref, cot_ref, y_ref, u_ref,
    db_ref, dc_ref, keep_ref, send_ref, arrived_ref, other_ref,
    mixed_ref, dinner_ref, dshared_ref, gstep_ref, rim_ref,
    reads, writes, ends, db_sum, dc_sum,
):
    k = pl.program_id(0)
    length = zv_ref.shape[0]
    groups = N // 8
    forward = edge_ref[2] == 0

    @pl.when(k == 0)
    def _():
        reads[...] = jnp.zeros_like(reads)
        writes[...] = jnp.zeros_like(writes)
        ends[...] = jnp.zeros_like(ends)
        db_sum[...] = db_ref[...]
        dc_sum[...] = dc_ref[...]

    zb = zb_ref[...]
    zc = zc_ref[...]
    sb = sigmoid(zb)
    sc = sigmoid(zc)
    b2 = split(zb * sb)
    c2 = split(zc * sc)
    lane = lax.broadcasted_iota(jnp.int32, (LANES, LANES), 1)
    row = lax.broadcasted_iota(jnp.int32, (LANES, LANES), 0)
    gather = jnp.where(lane == 2 * k + row // P_SIZE, 1.0, 0.0).astype(BF16)
    rows = pl.ds(pl.multiple_of(8 * k, 8), 8)
    arrived = arrived_ref[:, rows, :].reshape(N, LANES)
    other = other_ref[:, rows, :].reshape(N, LANES)
    keep = keep_ref[:, rows, :].reshape(N, LANES)
    send = send_ref[:, rows, :].reshape(N, LANES)
    state = jnp.where(forward, arrived, other)
    grad = jnp.where(forward, other, arrived)
    own = jnp.where(forward, keep, send)
    state2 = split(state)
    grad2 = split(grad)
    z = zv_ref[...]
    s = sigmoid(z)
    v = z * s
    g = cot_ref[...].astype(F32)
    cum = moving_tile(cum_ref[...], k)
    dt_k = moving_tile(dt_ref[...], k)
    skip = moving_tile(par_ref[...], k)[2:3, :]
    last = cum[length - 1 :, :]
    read_k = jnp.exp(cum)
    tail_k = jnp.exp(last - cum)
    y = y_ref[...] + read_k * dot3(c2, state2, NN)
    u = u_ref[...] + tail_k * dot3(b2, grad2, NN)
    mixed_ref[...] = (y + skip * v).astype(BF16)
    dv = dt_k * u + skip * g
    dinner = dv * (s * (1.0 + z * (1.0 - s)))
    dinner_ref[...] = dinner
    rim_ref[:, pl.ds(pl.multiple_of(k * LANES, LANES), LANES)] = dinner[0:8]
    reads[...] += dot2(split(g * y), gather, NN)
    writes[...] += dot2(split(v * u), gather, NN)
    dc_sum[...] += dot3(split(g * read_k), state2, NT)
    db_sum[...] += dot3(split(v * dt_k * tail_k), grad2, NT)
    end = jnp.sum(grad * (own + jnp.exp(last) * state), 0, keepdims=True)
    ends[...] += dot2(split(jnp.broadcast_to(end, (8, LANES))), gather, NN)

    @pl.when(k == tiles - 1)
    def _():
        dshared_ref[:, 0:LANES] = db_sum[...] * (sb * (1.0 + zb * (1.0 - sb)))
        dshared_ref[:, LANES:] = dc_sum[...] * (sc * (1.0 + zc * (1.0 - sc)))
        rim_ref[:, tiles * LANES :] = dshared_ref[0:8, :]
        grad_logs = triangle_sum(reads[...] - dt_ref[...] * writes[...], TN) + ends[0:1]
        grad_dt = writes[...] - par_ref[1:2, :] * grad_logs
        gstep_ref[...] = grad_dt * sigmoid(sp_ref[...])


def conv_back_kernel(
    edge_ref, dinner_ref, dshared_ref, rim_ref, ci_ref, cs_ref, gstep_ref,
    gi_ref, gst_ref, right_ref, wide_i, wide_s,
):
    length, inner = dinner_ref.shape
    shared = dshared_ref.shape[1]
    rim = rim_ref[...] * jnp.where(edge_ref[1] == 0, 1.0, 0.0)
    wide_i[0:length, :] = dinner_ref[...]
    wide_i[length:, :] = rim[:, 0:inner]
    wide_s[0:length, :] = dshared_ref[...]
    wide_s[length:, :] = rim[:, inner:]

    def back(wide, taps, k):
        at = slice(k * LANES, (k + 1) * LANES)
        out = taps[K - 1 : K, at] * wide[0:length, at]
        for j in range(1, K):
            out += taps[K - 1 - j : K - j, at] * wide[j : j + length, at]
        return out

    for k in range(shared // LANES):
        at = slice(k * LANES, (k + 1) * LANES)
        grad = jnp.transpose(back(wide_s, cs_ref, k))
        gst_ref[at, :] = grad
        high, low = split(grad)
        right_ref[inner + k * LANES : inner + (k + 1) * LANES, :] = high
        right_ref[inner + shared + k * LANES : inner + shared + (k + 1) * LANES, :] = low
    high, low = split(jnp.transpose(gstep_ref[...])[0:SLOT, :])
    right_ref[inner + 2 * shared : inner + 2 * shared + SLOT, :] = high
    right_ref[inner + 2 * shared + SLOT :, :] = low
    for k in range(inner // LANES):
        at = slice(k * LANES, (k + 1) * LANES)
        grad = back(wide_i, ci_ref, k)
        gi_ref[:, at] = grad.astype(BF16)
        right_ref[at, :] = jnp.transpose(grad).astype(BF16)


def token_grad_kernel(heads, wi_ref, ws_ref, wt_ref, right_ref, after_ref, out_ref, left):
    inner = wi_ref.shape[1]
    shared = ws_ref.shape[1]
    end = inner + 2 * shared
    left[:, 0:inner] = wi_ref[...]
    left[:, inner : inner + shared] = ws_ref[...]
    left[:, inner + shared : end] = ws_ref[...]
    blank = jnp.zeros((SLOT - heads, left.shape[0]), F32)
    step = jnp.concatenate([wt_ref[...].astype(F32), blank], 0)
    left[:, end:] = jnp.transpose(jnp.concatenate([step, step], 0)).astype(BF16)
    out_ref[...] = dot1(left[...], right_ref[...], NN).reshape(out_ref.shape)


def put_rows(edge_ref, product, mine_ref, other_ref):
    rows = mine_ref.shape[1] * mine_ref.shape[2] // RING
    parts = product.reshape(RING, CORES, rows, product.shape[1])

    def put(first, second):
        for z in range(RING):
            at = z * rows % mine_ref.shape[2]
            first[0, z * rows // mine_ref.shape[2], at : at + rows, :] = parts[z, 0]
            second[0, z * rows // mine_ref.shape[2], at : at + rows, :] = parts[z, 1]

    @pl.when(edge_ref[2] == 0)
    def _():
        put(mine_ref, other_ref)

    @pl.when(edge_ref[2] == 1)
    def _():
        put(other_ref, mine_ref)


def weight_grad_kernel(
    edge_ref, tok_ref, gi_ref, mine_a_ref, other_a_ref, mine_b_ref, other_b_ref
):
    product = dot1(tok_ref[...], gi_ref[...], TN)
    lanes = mine_a_ref.shape[3]
    put_rows(edge_ref, product[:, 0:lanes], mine_a_ref, other_a_ref)
    put_rows(edge_ref, product[:, lanes:], mine_b_ref, other_b_ref)


def side_grad_kernel(
    edge_ref, parts_ref, gstep_ref, tok_ref, after_ref, mine_ref, other_ref, right
):
    shared_cols = parts_ref.shape[1]

    @pl.when(pl.program_id(0) == 0)
    def _():
        total = parts_ref[0]
        for i in range(1, parts_ref.shape[0]):
            total += parts_ref[i]
        blank = jnp.zeros((LANES - shared_cols, total.shape[1]), F32)
        cols = jnp.transpose(jnp.concatenate([total, blank], 0))
        high, low = split(cols + pltpu.roll(gstep_ref[...], shared_cols, 1))
        right[:, 0:LANES] = high
        right[:, LANES:] = low

    both = dot1(tok_ref[...], right[...], TN)
    put_rows(edge_ref, both[:, 0:LANES] + both[:, LANES:], mine_ref, other_ref)


def ring_parts(place, part, up_ref, down_ref, hold_ref, own_ref):
    above, facing, below = [(place + i) % RING for i in (1, 2, 3)]
    up_ref[0] = part(facing, 0)
    up_ref[1] = part(above, 1)
    down_ref[0] = part(facing, 1)
    down_ref[1] = part(below, 0)
    hold_ref[0] = part(above, 0)
    hold_ref[1] = part(below, 1)
    own_ref[0] = part(place, 0)
    own_ref[1] = part(place, 1)


def core_sum_kernel(edge_ref, *refs):
    blocks = refs[:-5]
    up_ref, down_ref, hold_ref, own_ref = refs[-4:]

    def part(target, half):
        sums = [
            blocks[i][target, half] + blocks[i + 1][target, half]
            for i in range(0, len(blocks), 2)
        ]
        return jnp.concatenate(sums, 1) if len(sums) > 1 else sums[0]

    ring_parts(edge_ref[3], part, up_ref, down_ref, hold_ref, own_ref)


def pass_on_kernel(hold_ref, from_below_ref, from_above_ref, after_ref, up_ref, down_ref):
    up_ref[...] = hold_ref[0] + from_below_ref[0]
    down_ref[...] = hold_ref[1] + from_above_ref[0]


def ring_sum(own_ref, from_below_ref, from_above_ref, last_below_ref, last_above_ref):
    first = own_ref[0] + from_above_ref[1] + last_below_ref[...]
    second = own_ref[1] + from_below_ref[1] + last_above_ref[...]
    return first, second


def next_ring_kernel(
    edge_ref, own_in, from_below_ref, from_above_ref, last_below_ref, last_above_ref, after_ref,
    up_ref, down_ref, hold_ref, own_ref, sums,
):
    first, second = ring_sum(
        own_in, from_below_ref, from_above_ref, last_below_ref, last_above_ref
    )
    half = RING // 2
    shape = (half,) + sums.shape[1:]
    sums[0:half] = first.reshape(shape)
    sums[half:] = second.reshape(shape)

    def part(target, which):
        return sums[target, which]

    ring_parts(edge_ref[4], part, up_ref, down_ref, hold_ref, own_ref)


def last_ring_kernel(*refs):
    inner_ref, shared_ref, step_ref, side = refs[10:]
    half = inner_ref.shape[0] // 2
    at = (slice(0, half), slice(half, 2 * half))
    lanes = refs[0].shape[2]
    shared_cols = shared_ref.shape[0]
    rest = inner_ref.shape[1] - lanes
    side[2 * half :, :] = jnp.zeros((side.shape[0] - 2 * half, LANES), F32)
    for rows, part in zip(at, ring_sum(*refs[0:5])):
        inner_ref[rows, 0:lanes] = part
    for rows, part in zip(at, ring_sum(*refs[5:10])):
        inner_ref[rows, lanes:] = part[:, 0:rest]
        side[rows, :] = part[:, rest:]
    flat = jnp.transpose(side[...])
    shared_ref[...] = flat[0:shared_cols, 0 : 2 * half]
    step_ref[...] = flat[shared_cols : shared_cols + step_ref.shape[0], 0 : 2 * half]


def sum_kernel(parts_ref, out_ref):
    total = parts_ref[0]
    for i in range(1, parts_ref.shape[0]):
        total += parts_ref[i]
    out_ref[...] = total.astype(out_ref.dtype)


def whole(shape):
    return pl.BlockSpec(shape, lambda *_: (0,) * len(shape))


def after():
    return pl.BlockSpec(memory_space=pl.ANY)


def smem():
    return pl.BlockSpec(memory_space=pltpu.SMEM)


def body(
    tokens,
    inner_weight,
    shared_weight,
    step_weight,
    conv_inner,
    conv_shared,
    step_bias,
    decay_rate,
    skip_gain,
    cotangent,
):
    length, width = tokens.shape
    inner = inner_weight.shape[1]
    shared = shared_weight.shape[1]
    heads = step_weight.shape[1]
    tiles = inner // LANES
    ctx = lax.axis_size("ctx")
    tp = lax.axis_size("tp")
    place = lax.axis_index("ctx")
    core = place % CORES
    z_place = place // CORES % RING
    y_place = place // (CORES * RING)
    edge = jnp.stack([place, (place == ctx - 1).astype(jnp.int32), core, y_place, z_place])
    edge = edge.astype(jnp.int32)
    chips = ctx // CORES
    same_core = [[CORES * chip + i for chip in range(chips)] for i in range(CORES)]
    sds = jax.ShapeDtypeStruct
    step_weight_t = step_weight.T

    rim = shifted(tokens[length - 8 :].astype(F32), "ctx", 1)
    params = jnp.pad(
        jnp.stack([step_bias, decay_rate, skip_gain]), ((0, 5), (0, LANES - heads))
    )

    block = 512
    total = inner + shared
    pay_rows = 8 * tiles + 8
    z, sp, dt, cum, cum_t, keep, send = pl.pallas_call(
        functools.partial(project_kernel, tiles, heads),
        grid=(width // block,),
        in_specs=[
            smem(),
            pl.BlockSpec((length, block), lambda i: (0, i)),
            pl.BlockSpec((8, block), lambda i: (0, i)),
            pl.BlockSpec((block, inner), lambda i: (i, 0)),
            pl.BlockSpec((block, shared), lambda i: (i, 0)),
            pl.BlockSpec((heads, block), lambda i: (0, i)),
            whole((K, inner)),
            whole((K, shared)),
            whole((8, LANES)),
            whole((length, inner)),
        ],
        out_specs=[
            whole((length, total)),
            whole((length, LANES)),
            whole((length, LANES)),
            whole((length, LANES)),
            whole((SLOT, length)),
            whole((chips, pay_rows, LANES)),
            whole((chips, pay_rows, LANES)),
        ],
        out_shape=[
            sds((length, total), F32),
            sds((length, LANES), F32),
            sds((length, LANES), F32),
            sds((length, LANES), F32),
            sds((SLOT, length), F32),
            sds((chips, pay_rows, LANES), F32),
            sds((chips, pay_rows, LANES), F32),
        ],
        scratch_shapes=[
            pltpu.VMEM((length + 16, block), BF16),
            pltpu.VMEM((length + 16, inner), F32),
            pltpu.VMEM((length + 16, shared), F32),
            pltpu.VMEM((length + 16, LANES), F32),
        ],
        compiler_params=PARAMS,
        name="project",
    )(
        edge, tokens, rim, inner_weight, shared_weight, step_weight_t,
        conv_inner, conv_shared, params, cotangent,
    )

    got = ctx_shift(send, 0, 0, 1)
    chip_state = pl.pallas_call(
        functools.partial(chip_kernel, tiles),
        out_shape=sds((chips, pay_rows, LANES), F32),
        compiler_params=PARAMS,
        name="chip_state",
    )(keep, got)
    by_rows = lax.all_to_all(
        chip_state, "ctx", 0, 0, axis_index_groups=same_core, tiled=True
    )

    y, u, db, dc = pl.pallas_call(
        local_kernel,
        grid=(tiles,),
        in_specs=[
            pl.BlockSpec((length, LANES), lambda i: (0, i)),
            pl.BlockSpec((length, LANES), lambda i: (0, tiles)),
            pl.BlockSpec((length, LANES), lambda i: (0, tiles + 1)),
            whole((length, LANES)),
            whole((length, LANES)),
            whole((SLOT, length)),
            pl.BlockSpec((length, LANES), lambda i: (0, i)),
        ],
        out_specs=[
            pl.BlockSpec((length, LANES), lambda i: (0, i)),
            pl.BlockSpec((length, LANES), lambda i: (0, i)),
            whole((length, LANES)),
            whole((length, LANES)),
        ],
        out_shape=[
            sds((length, inner), F32),
            sds((length, inner), F32),
            sds((length, LANES), F32),
            sds((length, LANES), F32),
        ],
        scratch_shapes=[
            pltpu.VMEM((2, length // 2, length // 2), F32),
            pltpu.VMEM((2, length // 2, length // 2), F32),
            pltpu.VMEM((length, LANES), F32),
            pltpu.VMEM((length, LANES), F32),
        ],
        compiler_params=PARAMS,
        cost_estimate=pl.CostEstimate(
            flops=10 * length * length * inner, bytes_accessed=8_000_000, transcendentals=0
        ),
        name="local",
    )(z, z, z, dt, cum, cum_t, cotangent)

    scanned = pl.pallas_call(
        functools.partial(ctx_scan_kernel, tiles),
        in_specs=[smem(), whole((chips, pay_rows, LANES)), after()],
        out_specs=whole((chips, 8 * tiles, LANES)),
        out_shape=sds((chips, 8 * tiles, LANES), F32),
        compiler_params=PARAMS,
        name="ctx_scan",
    )(edge, by_rows, dc)
    arrived = lax.all_to_all(scanned, "ctx", 0, 0, axis_index_groups=same_core, tiled=True)
    onward = pl.pallas_call(
        functools.partial(onward_kernel, tiles),
        out_shape=sds((chips, 8 * tiles, LANES), F32),
        compiler_params=PARAMS,
        name="onward",
    )(keep, arrived)
    other = ctx_shift(onward, 0, 0, 1)

    tile = pl.BlockSpec((length, LANES), lambda i: (0, i))
    column = whole((length, LANES))
    mixed, dinner, dshared, gstep, rim_out = pl.pallas_call(
        functools.partial(join_kernel, tiles),
        grid=(tiles,),
        in_specs=[
            smem(),
            tile,
            pl.BlockSpec((length, LANES), lambda i: (0, tiles)),
            pl.BlockSpec((length, LANES), lambda i: (0, tiles + 1)),
            column,
            column,
            column,
            whole((8, LANES)),
            tile,
            tile,
            tile,
            column,
            column,
            whole((chips, pay_rows, LANES)),
            whole((chips, pay_rows, LANES)),
            whole((chips, 8 * tiles, LANES)),
            whole((chips, 8 * tiles, LANES)),
        ],
        out_specs=[tile, tile, whole((length, shared)), column, whole((8, total))],
        out_shape=[
            sds((length, inner), BF16),
            sds((length, inner), F32),
            sds((length, shared), F32),
            sds((length, LANES), F32),
            sds((8, total), F32),
        ],
        scratch_shapes=[
            pltpu.VMEM((length, LANES), F32),
            pltpu.VMEM((length, LANES), F32),
            pltpu.VMEM((8, LANES), F32),
            pltpu.VMEM((length, LANES), F32),
            pltpu.VMEM((length, LANES), F32),
        ],
        compiler_params=PARAMS,
        name="join",
    )(
        edge, z, z, z, sp, dt, cum, params, cotangent, y, u, db, dc,
        keep, send, arrived, other,
    )

    rim_back = shifted(rim_out, "ctx", -1)
    right_rows = inner + 2 * shared + 2 * SLOT
    grad_inner, grad_shared_t, right = pl.pallas_call(
        conv_back_kernel,
        in_specs=[
            smem(),
            whole((length, inner)),
            whole((length, shared)),
            whole((8, total)),
            whole((K, inner)),
            whole((K, shared)),
            column,
        ],
        out_specs=[
            whole((length, inner)), whole((shared, length)), whole((right_rows, length)),
        ],
        out_shape=[
            sds((length, inner), BF16),
            sds((shared, length), F32),
            sds((right_rows, length), BF16),
        ],
        scratch_shapes=[
            pltpu.VMEM((length + 8, inner), F32),
            pltpu.VMEM((length + 8, shared), F32),
        ],
        compiler_params=PARAMS,
        name="conv_back",
    )(edge, dinner, dshared, rim_back, conv_inner, conv_shared, gstep)

    shared_cols = shared // tp
    shared_parts = lax.all_to_all(
        grad_shared_t.reshape(tp, shared_cols, length), "tp", 0, 0, tiled=True
    )

    rows = width // ctx
    y_half = RING * rows // 2
    z_half = rows // 2
    lanes = (inner + LANES) // 2
    rest = inner - lanes

    def row_block(wide):
        return pl.BlockSpec((1, 2, y_half, wide), lambda i: (i, 0, 0, 0))

    def row_shape(wide):
        return sds((RING, 2, y_half, wide), F32)

    mine, other_a, mine_b, other_b = pl.pallas_call(
        weight_grad_kernel,
        grid=(RING,),
        in_specs=[
            smem(),
            pl.BlockSpec((length, width // RING), lambda i: (0, i)),
            whole((length, inner)),
        ],
        out_specs=[row_block(lanes)] * 2 + [row_block(rest)] * 2,
        out_shape=[row_shape(lanes)] * 2 + [row_shape(rest)] * 2,
        compiler_params=PARAMS,
        name="weight_grad",
    )(edge, tokens, grad_inner)
    got_a = ctx_shift(other_a, 0, 0, 1)
    got_b = ctx_shift(other_b, 0, 0, 1)

    cols = width // tp
    per = 2
    token_parts = pl.pallas_call(
        functools.partial(token_grad_kernel, heads),
        grid=(tp // per,),
        in_specs=[
            pl.BlockSpec((per * cols, inner), lambda i: (i, 0)),
            pl.BlockSpec((per * cols, shared), lambda i: (i, 0)),
            pl.BlockSpec((heads, per * cols), lambda i: (0, i)),
            whole((right_rows, length)),
            after(),
        ],
        out_specs=pl.BlockSpec((per, cols, length), lambda i: (i, 0, 0)),
        out_shape=sds((tp, cols, length), F32),
        scratch_shapes=[pltpu.VMEM((per * cols, right_rows), BF16)],
        compiler_params=PARAMS,
        name="token_grad",
    )(inner_weight, shared_weight, step_weight_t, right, mine)
    token_got = lax.all_to_all(token_parts, "tp", 0, 0, tiled=True)

    def core_sum(blocks, ready):
        return pl.pallas_call(
            core_sum_kernel,
            in_specs=[smem()] + [whole(block.shape) for block in blocks] + [after()],
            out_specs=[whole((2, y_half, lanes))] * 4,
            out_shape=[sds((2, y_half, lanes), F32)] * 4,
            compiler_params=PARAMS,
            name="core_sum",
        )(edge, *blocks, ready)

    def exchange(up, down, dy, dz):
        return ctx_shift(up, dy, dz, 0), ctx_shift(down, -dy, -dz, 0)

    def pass_on(hold, below, above, ready):
        half = hold.shape[1]
        return pl.pallas_call(
            pass_on_kernel,
            in_specs=[whole(hold.shape)] * 3 + [after()],
            out_specs=[whole((half, lanes))] * 2,
            out_shape=[sds((half, lanes), F32)] * 2,
            compiler_params=PARAMS,
            name="pass_on",
        )(hold, below, above, ready)

    def next_ring(own, below, above, last_below, last_above, ready):
        return pl.pallas_call(
            next_ring_kernel,
            in_specs=[smem()]
            + [whole((2, y_half, lanes))] * 3
            + [whole((y_half, lanes))] * 2
            + [after()],
            out_specs=[whole((2, z_half, lanes))] * 4,
            out_shape=[sds((2, z_half, lanes), F32)] * 4,
            scratch_shapes=[pltpu.VMEM((RING, 2, z_half, lanes), F32)],
            compiler_params=PARAMS,
            name="next_ring",
        )(edge, own, below, above, last_below, last_above, ready)

    up_a, down_a, hold_a, own_a = core_sum((mine, got_a), token_parts)
    first_a = exchange(up_a, down_a, 1, 0)
    side_mine, side_other = pl.pallas_call(
        side_grad_kernel,
        grid=(RING,),
        in_specs=[
            smem(),
            whole((tp, shared_cols, length)),
            column,
            pl.BlockSpec((length, width // RING), lambda i: (0, i)),
            after(),
        ],
        out_specs=[row_block(LANES)] * 2,
        out_shape=[row_shape(LANES)] * 2,
        scratch_shapes=[pltpu.VMEM((length, 2 * LANES), BF16)],
        compiler_params=PARAMS,
        name="side_grad",
    )(edge, shared_parts, gstep, tokens, hold_a)
    side_got = ctx_shift(side_other, 0, 0, 1)
    up_b, down_b, hold_b, own_b = core_sum((mine_b, got_b, side_mine, side_got), hold_a)
    first_b = exchange(up_b, down_b, 1, 0)
    up_a, down_a = pass_on(hold_a, *first_a, hold_b)
    second_a = exchange(up_a, down_a, 1, 0)
    up_b, down_b = pass_on(hold_b, *first_b, up_a)
    second_b = exchange(up_b, down_b, 1, 0)
    up_a, down_a, hold_a, own_a = next_ring(own_a, *first_a, *second_a, up_b)
    first_a = exchange(up_a, down_a, 0, 1)
    up_b, down_b, hold_b, own_b = next_ring(own_b, *first_b, *second_b, hold_a)
    first_b = exchange(up_b, down_b, 0, 1)
    up_a, down_a = pass_on(hold_a, *first_a, hold_b)
    second_a = exchange(up_a, down_a, 0, 1)
    up_b, down_b = pass_on(hold_b, *first_b, up_a)
    second_b = exchange(up_b, down_b, 0, 1)
    grad_inner_weight, grad_shared_weight, grad_step_weight = pl.pallas_call(
        last_ring_kernel,
        out_shape=[
            sds((rows, inner), F32),
            sds((shared_cols, rows), F32),
            sds((heads, rows), F32),
        ],
        scratch_shapes=[pltpu.VMEM((LANES, LANES), F32)],
        compiler_params=PARAMS,
        name="last_ring",
    )(own_a, *first_a, *second_a, own_b, *first_b, *second_b)

    grad_tokens = pl.pallas_call(
        sum_kernel,
        out_shape=sds((cols, length), BF16),
        compiler_params=PARAMS,
        name="token_sum",
    )(token_got)
    return (
        mixed,
        grad_tokens.T,
        grad_inner_weight,
        grad_shared_weight.T,
        grad_step_weight.T,
    )


def solution(mesh):
    in_specs = (
        P("ctx", None),
        P(None, "tp"),
        P(),
        P(None, "tp"),
        P(None, "tp"),
        P(),
        P("tp"),
        P("tp"),
        P("tp"),
        P("ctx", "tp"),
    )
    out_specs = (P("ctx", "tp"), P("ctx", "tp"), P("ctx", "tp"), P("ctx", "tp"), P("ctx", "tp"))
    return jax.shard_map(body, mesh=mesh, in_specs=in_specs, out_specs=out_specs, check_vma=False)
```

time: 282 us -> 218 us (0.77)
  waiting for transfers between devices: 105 us -> 31.9 us
  Pallas kernels: 52.3 us -> 90.4 us
  starting transfers between devices: 22.7 us -> 55.3 us
  blocking collectives: 49.8 us -> 21.1 us
  local copies, waits for them, and re-layouts: 32.7 us -> 14.1 us
  between operations: 14.2 us -> 0.77 us
    all_to_all x3, waiting for transfers between devices: 91.1 us -> 0.73 us  [the longest x1 0.72 us: body(): lax.all_to_all(chip_state, 'ctx', 0, 0, axis_index_groups=same_core, tile...]
    pallas_call x6 -> x17, Pallas kernels: 28.6 us -> 62.3 us  [the longest x1 10.1 us: body(): pl.pallas_call(functools.partial(join_kernel, tiles), grid=(tiles,), in_s...]
    ppermute x0 -> x21, starting transfers between devices: none -> 33.6 us  [ctx_shift(): return lax.ppermute(block, 'ctx', route)]
    all_to_all x2 -> x1, blocking collectives: 49.8 us -> 21.1 us  [body(): lax.all_to_all(scanned, 'ctx', 0, 0, axis_index_groups=same_core, tiled=T...]
    ppermute x0 -> x21, waiting for transfers between devices: none -> 27.2 us  [ctx_shift(): return lax.ppermute(block, 'ctx', route)]
    unnamed x70 -> x54, local copies, waits for them, and re-layouts: 25.7 us -> 13.5 us
    reduce_scatter x1 -> x0, waiting for transfers between devices: 10.5 us -> none  [body(): lax.psum_scatter(weight_parts, 'ctx', scatter_dimension=0, tiled=False)]
    reshape x2 -> x0, local copies, waits for them, and re-layouts: 4.85 us -> none  [body(): side = jnp.transpose(side.reshape(side_rows, ctx, rows), (1, 0, 2))]
  transfers between devices with their start and end apart: 6 -> 26, of which waited for: 5 -> 10; matrix products, arithmetic and copies ran while one was open for 2% -> 1% of each run, Pallas kernels for 11% -> 25%
where the time goes in v2:
time: 218 us; the launch traced here: 216 us
  Pallas kernels  90.4 us (41%)
  starting transfers between devices  55.3 us (25%)
  waiting for transfers between devices  31.9 us (15%)
  blocking collectives  21.1 us (10%)
  local copies, waits for them, and re-layouts  14.1 us (6%)
    ppermute x21, starting transfers between devices, ctx_shift(): return lax.ppermute(block, 'ctx', route)  33.6 us
    ppermute x21, waiting for transfers between devices, ctx_shift(): return lax.ppermute(block, 'ctx', route)  27.2 us
    all_to_all x1, blocking collectives, body(): lax.all_to_all(scanned, 'ctx', 0, 0, axis_index_groups=same_core, tiled=T...  21.1 us
    unnamed x54, local copies, waits for them, and re-layouts  13.5 us
    pallas_call x1, Pallas kernels, body(): pl.pallas_call(functools.partial(project_kernel, tiles, heads), grid=(wid...  13.3 us
    pallas_call x1, Pallas kernels, body(): pl.pallas_call(local_kernel, grid=(tiles,), in_specs=[pl.BlockSpec((lengt...  12.9 us
    pallas_call x1, Pallas kernels, body(): pl.pallas_call(functools.partial(join_kernel, tiles), grid=(tiles,), in_s...  10.1 us
    pallas_call x1, Pallas kernels, body(): pl.pallas_call(functools.partial(token_grad_kernel, heads), grid=(tp // p...  7.79 us
  transfers between devices with their start and end apart: 26, of which 10 were waited for; matrix products, arithmetic and copies ran while one was open for 1% of the time, Pallas kernels for 25%

profile of v2, /device:TPU:1, one launch (start us, length us, event | category | flops | bytes accessed | tf_op | source)
XLA Modules:
  0.0 215.6 jit_solution(13961416159305938918)
XLA Ops:
  1.4 4.4 %collective-permute-start = (f32[8,2560]{1,0:T(8,128)S(1)}, f32[8,2560]{1,0:T(8,128)S(1)}, u32[]{:S(2)}, u32[]{:S(2)}) collective-permute-start(f32[8,2560]{1,0:T(8,128)S(1)} %slice_convert_fusion), channel_id=1, source_target_pairs={{0,8},{8,16},{16,24},{24,32},{32,40},{40,48},{48,56},{56,64},{64,7... | collective-permute-start | bytes 245768 | tf_op jit(solution)/shard_map/ppermute | solution.py:27
  6.4 1.3 select_maximum_fusion.par_ref
  8.4 13.3 %project.1 = (f32[512,896]{1,0:T(8,128)}, f32[512,128]{1,0:T(8,128)}, f32[512,128]{1,0:T(8,128)}, f32[512,128]{1,0:T(8,128)}, f32[16,512]{1,0:T(8,128)}, /*index=5*/f32[16,48,128]{2,1,0:T(8,128)}, f32[16,48,128]{2,1,0:T(8,128)}) custom-call(s32[5]{0:T(128)} %stack.39.edge_ref, bf16[512,2560]{1,0:T(8,128)(2,1)} %tok_ref.5, f32[8,2560]{1,0:T(8,128)} %copy-done.19, ...), custom_call_target="tpu_custom_call" | custom-call | tf_op jit(solution)/shard_map/project/pallas_call | solution.py:598
  21.6 5.6 %collective-permute-start.1 = (f32[16,48,128]{2,1,0:T(8,128)}, f32[16,48,128]{2,1,0:T(8,128)S(1)}, u32[]{:S(2)}, u32[]{:S(2)}) collective-permute-start(f32[16,48,128]{2,1,0:T(8,128)} %get-tuple-element.67.send_ref), channel_id=1, source_target_pairs={{0,8},{8,0},{16,24},{24,16},{32,40},{40,32},{48,56},{56,48},{64,72... | collective-permute-start | bytes 1179656 | tf_op jit(solution)/shard_map/ppermute | solution.py:40
  27.3 1.6 collective-permute-done.1.got_ref
  29.6 1.9 chip_state.1
  31.5 6.6 %all-to-all-start = ((f32[16,48,128]{2,1,0:T(8,128)}), f32[16,48,128]{2,1,0:T(8,128)S(1)}, u32[]{:S(2)}, u32[]{:S(2)}) async-start(f32[16,48,128]{2,1,0:T(8,128)} %chip_state.1), calls=%async_computation | async-start | bytes 786432 | tf_op jit(solution)/shard_map/all_to_all | solution.py:651
  38.1 12.9 %local.1 = (f32[512,640]{1,0:T(8,128)}, f32[512,640]{1,0:T(8,128)}, f32[512,128]{1,0:T(8,128)}, f32[512,128]{1,0:T(8,128)}) custom-call(f32[512,896]{1,0:T(8,128)} %get-tuple-element.57.zv_ref.zb_ref.zc_ref, f32[512,896]{1,0:T(8,128)} %get-tuple-element.57.zv_ref.zb_ref.zc_ref, f32[512,896]{1,0:T(8,128)} %get-tuple-element.57.zv_ref.zb_ref.zc_ref, ...), custom_call_target="tpu_custom_call" | custom-call | flops 1677721600 | bytes 8000000 | tf_op jit(solution)/shard_map/local/pallas_call | solution.py:655
  52.5 1.8 ctx_scan.1
  54.3 21.1 %all_to_all.20.arrived_ref = f32[16,40,128]{2,1,0:T(8,128)} all-to-all(f32[16,40,128]{2,1,0:T(8,128)} %ctx_scan.1), channel_id=1, replica_groups={{0,16,32,48,64,80,96,112,128,144,160,176,192,208,224,240},{8,24,40,56,7..., dimensions={0} | all-to-all | bytes 655360 | tf_op jit(solution)/shard_map/all_to_all | solution.py:700
  75.4 1.9 onward.1
  77.3 2.8 %collective-permute-start.2 = (f32[16,40,128]{2,1,0:T(8,128)}, f32[16,40,128]{2,1,0:T(8,128)S(1)}, u32[]{:S(2)}, u32[]{:S(2)}) collective-permute-start(f32[16,40,128]{2,1,0:T(8,128)} %onward.1), channel_id=1, source_target_pairs={{0,8},{8,0},{16,24},{24,16},{32,40},{40,32},{48,56},{56,48},{64,72... | collective-permute-start | bytes 983048 | tf_op jit(solution)/shard_map/ppermute | solution.py:40
  80.1 1.5 collective-permute-done.2.other_ref
  82.3 10.1 %join.1 = (bf16[512,640]{1,0:T(8,128)(2,1)}, f32[512,640]{1,0:T(8,128)}, f32[512,256]{1,0:T(8,128)}, f32[512,128]{1,0:T(8,128)}, f32[8,896]{1,0:T(8,128)}) custom-call(s32[5]{0:T(128)} %stack.39.edge_ref, f32[512,896]{1,0:T(8,128)} %get-tuple-element.57.zv_ref.zb_ref.zc_ref, f32[512,896]{1,0:T(8,128)} %get-tuple-element.57.zv_ref.zb_ref.zc_ref, ...), custom_call_target="tpu_custom_call" | custom-call | tf_op jit(solution)/shard_map/join/pallas_call | solution.py:711
  92.9 4.0 %collective-permute-done.3.rim_ref = f32[8,896]{1,0:T(8,128)S(1)} collective-permute-done((f32[8,896]{1,0:T(8,128)}, f32[8,896]{1,0:T(8,128)S(1)}, u32[]{:S(2)}, u32[]{:S(2)}) %collective-permute-start.3) | collective-permute-done | bytes 28704 | tf_op jit(solution)/shard_map/ppermute | solution.py:27
  97.5 3.8 %conv_back.1 = (bf16[512,640]{1,0:T(8,128)(2,1)}, f32[256,512]{1,0:T(8,128)}, bf16[1184,512]{1,0:T(8,128)(2,1)}) custom-call(s32[5]{0:T(128)} %stack.39.edge_ref, f32[512,640]{1,0:T(8,128)} %get-tuple-element.69.dinner_ref, f32[512,256]{1,0:T(8,128)} %get-tuple-element.70.dshared_ref, f32[8,896]{1,0:T(8,128)} %copy-done.24, f32[4,640]{1,0:T(4,128)} %ci_ref.3, ...), custom_call_target="tpu_custom_call" | custom-call | tf_op jit(solution)/shard_map/conv_back/pallas_call | solution.py:757
  101.3 5.1 %all-to-all-start.3 = ((f32[8,32,512]{2,1,0:T(8,128)}), f32[8,32,512]{2,1,0:T(8,128)S(1)}, u32[]{:S(2)}, u32[]{:S(2)}) async-start(f32[8,32,512]{2,1,0:T(8,128)} %bitcast.13), calls=%async_computation.3 | async-start | bytes 1048576 | tf_op jit(solution)/shard_map/all_to_all | solution.py:785
  106.4 6.8 %weight_grad.1 = (f32[4,2,160,384]{3,2,1,0:T(8,128)}, f32[4,2,160,384]{3,2,1,0:T(8,128)}, f32[4,2,160,256]{3,2,1,0:T(8,128)}, f32[4,2,160,256]{3,2,1,0:T(8,128)}) custom-call(s32[5]{0:T(128)} %stack.39.edge_ref, bf16[512,2560]{1,0:T(8,128)(2,1)} %tok_ref.5, bf16[512,640]{1,0:T(8,128)(2,1)} %get-tuple-element.74.gi_ref), custom_call_target="tpu_custom_call" | custom-call | tf_op jit(solution)/shard_map/weight_grad/pallas_call | solution.py:801
  113.3 7.8 %token_grad.1.refs_2_ = f32[8,320,512]{2,1,0:T(8,128)} custom-call(bf16[2560,640]{1,0:T(8,128)(2,1)} %wi_ref.3, bf16[2560,256]{1,0:T(8,128)(2,1)} %ws_ref.3, bf16[10,2560]{1,0:T(8,128)(2,1)} %bitcast.15, bf16[1184,512]{1,0:T(8,128)(2,1)} %get-tuple-element.73.right_ref, f32[4,2,160,384]{3,2,1,0:T(8,128)} %get-tuple-element.75.after_ref.refs_0_), custom_call_target="tpu_custom_call" | custom-call | tf_op jit(solution)/shard_map/token_grad/pallas_call | solution.py:819
  121.9 5.1 %all-to-all-start.2 = ((f32[8,320,512]{2,1,0:T(8,128)}), f32[8,320,512]{2,1,0:T(8,128)}, u32[]{:S(2)}, u32[]{:S(2)}) async-start(f32[8,320,512]{2,1,0:T(8,128)} %token_grad.1.refs_2_), calls=%async_computation.2 | async-start | bytes 10485760 | tf_op jit(solution)/shard_map/all_to_all | solution.py:835
  127.5 3.7 %collective-permute-done.4.refs_1_ = f32[4,2,160,384]{3,2,1,0:T(8,128)S(1)} collective-permute-done((f32[4,2,160,384]{3,2,1,0:T(8,128)}, f32[4,2,160,384]{3,2,1,0:T(8,128)S(1)}, u32[]{:S(2)}, u32[]{:S(2)}) %collective-permute-start.4) | collective-permute-done | bytes 1966112 | tf_op jit(solution)/shard_map/ppermute | solution.py:40
  131.2 1.3 copy-done.1
  132.4 3.6 %core_sum.2 = (f32[2,160,384]{2,1,0:T(8,128)}, f32[2,160,384]{2,1,0:T(8,128)}, f32[2,160,384]{2,1,0:T(8,128)}, f32[2,160,384]{2,1,0:T(8,128)}) custom-call(s32[5]{0:T(128)} %stack.39.edge_ref, f32[4,2,160,384]{3,2,1,0:T(8,128)} %get-tuple-element.75.after_ref.refs_0_, f32[4,2,160,384]{3,2,1,0:T(8,128)} %copy-done.1, f32[8,320,512]{2,1,0:T(8,128)} %token_grad.1.refs_2_), custom_call_target="tpu_custom_call" | custom-call | tf_op jit(solution)/shard_map/core_sum/pallas_call | solution.py:838
  136.1 5.1 %side_grad.1 = (f32[4,2,160,128]{3,2,1,0:T(8,128)}, f32[4,2,160,128]{3,2,1,0:T(8,128)}) custom-call(s32[5]{0:T(128)} %stack.39.edge_ref, f32[8,32,512]{2,1,0:T(8,128)} %copy-done, f32[512,128]{1,0:T(8,128)} %get-tuple-element.72.gstep_ref, bf16[512,2560]{1,0:T(8,128)(2,1)} %tok_ref.5, f32[2,160,384]{2,1,0:T(8,128)} %get-tuple-element.80.after_ref.refs_4_.hold_ref), custom_call_target="tpu_custom_call" | custom-call | tf_op jit(solution)/shard_map/side_grad/pallas_call | solution.py:877
  141.5 2.4 %collective-permute-start.6 = (f32[2,160,384]{2,1,0:T(8,128)S(1)}, f32[2,160,384]{2,1,0:T(8,128)S(1)}, u32[]{:S(2)}, u32[]{:S(2)}) collective-permute-start(f32[2,160,384]{2,1,0:T(8,128)S(1)} %copy-done.25), channel_id=1, source_target_pairs={{0,192},{8,200},{16,208},{24,216},{32,224},{40,232},{48,240},{56,2... | collective-permute-start | bytes 1474568 | tf_op jit(solution)/shard_map/ppermute | solution.py:40
  144.0 1.1 copy-done.7
  145.2 3.5 %core_sum.3 = (f32[2,160,384]{2,1,0:T(8,128)}, f32[2,160,384]{2,1,0:T(8,128)}, f32[2,160,384]{2,1,0:T(8,128)}, f32[2,160,384]{2,1,0:T(8,128)}) custom-call(s32[5]{0:T(128)} %stack.39.edge_ref, f32[4,2,160,256]{3,2,1,0:T(8,128)} %get-tuple-element.81.refs_0_, f32[4,2,160,256]{3,2,1,0:T(8,128)} %copy-done.7, f32[4,2,160,128]{3,2,1,0:T(8,128)} %get-tuple-element.84.refs_2_, ...), custom_call_target="tpu_custom_call" | custom-call | tf_op jit(solution)/shard_map/core_sum/pallas_call | solution.py:838
  148.8 2.7 %collective-permute-start.12 = (f32[2,160,384]{2,1,0:T(8,128)}, f32[2,160,384]{2,1,0:T(8,128)S(1)}, u32[]{:S(2)}, u32[]{:S(2)}) collective-permute-start(f32[2,160,384]{2,1,0:T(8,128)} %get-tuple-element.90), channel_id=1, source_target_pairs={{0,192},{8,200},{16,208},{24,216},{32,224},{40,232},{48,240},{56,2... | collective-permute-start | bytes 1474568 | tf_op jit(solution)/shard_map/ppermute | solution.py:40
  151.5 3.5 %collective-permute-done.5.from_below_ref = f32[2,160,384]{2,1,0:T(8,128)S(1)} collective-permute-done((f32[2,160,384]{2,1,0:T(8,128)S(1)}, f32[2,160,384]{2,1,0:T(8,128)S(1)}, u32[]{:S(2)}, u32[]{:S(2)}) %collective-permute-start.5) | collective-permute-done | bytes 491552 | tf_op jit(solution)/shard_map/ppermute | solution.py:40
  156.0 2.1 pass_on.4
  158.2 2.2 %collective-permute-start.10 = (f32[160,384]{1,0:T(8,128)}, f32[160,384]{1,0:T(8,128)S(1)}, u32[]{:S(2)}, u32[]{:S(2)}) collective-permute-start(f32[160,384]{1,0:T(8,128)} %get-tuple-element.88), channel_id=1, source_target_pairs={{0,192},{8,200},{16,208},{24,216},{32,224},{40,232},{48,240},{56,2... | collective-permute-start | bytes 737288 | tf_op jit(solution)/shard_map/ppermute | solution.py:40
  160.3 5.2 %collective-permute-done.11.from_below_ref = f32[2,160,384]{2,1,0:T(8,128)S(1)} collective-permute-done((f32[2,160,384]{2,1,0:T(8,128)}, f32[2,160,384]{2,1,0:T(8,128)S(1)}, u32[]{:S(2)}, u32[]{:S(2)}) %collective-permute-start.11) | collective-permute-done | bytes 491552 | tf_op jit(solution)/shard_map/ppermute | solution.py:40
  167.1 2.1 pass_on.5
  169.2 2.7 %collective-permute-start.16 = (f32[160,384]{1,0:T(8,128)}, f32[160,384]{1,0:T(8,128)S(1)}, u32[]{:S(2)}, u32[]{:S(2)}) collective-permute-start(f32[160,384]{1,0:T(8,128)} %get-tuple-element.97), channel_id=1, source_target_pairs={{0,192},{8,200},{16,208},{24,216},{32,224},{40,232},{48,240},{56,2... | collective-permute-start | bytes 737288 | tf_op jit(solution)/shard_map/ppermute | solution.py:40
  172.7 2.4 %next_ring.2 = (f32[2,40,384]{2,1,0:T(8,128)}, f32[2,40,384]{2,1,0:T(8,128)}, f32[2,40,384]{2,1,0:T(8,128)}, f32[2,40,384]{2,1,0:T(8,128)}) custom-call(s32[5]{0:T(128)} %stack.39.edge_ref, f32[2,160,384]{2,1,0:T(8,128)} %get-tuple-element.77.own_in, f32[2,160,384]{2,1,0:T(8,128)} %copy-done.3, f32[2,160,384]{2,1,0:T(8,128)} %copy-done.5, ...), custom_call_target="tpu_custom_call" | custom-call | tf_op jit(solution)/shard_map/next_ring/pallas_call | solution.py:862
  175.0 1.3 collective-permute-start.13
  176.3 2.3 %collective-permute-start.14 = (f32[2,40,384]{2,1,0:T(8,128)}, f32[2,40,384]{2,1,0:T(8,128)S(1)}, u32[]{:S(2)}, u32[]{:S(2)}) collective-permute-start(f32[2,40,384]{2,1,0:T(8,128)} %get-tuple-element.94), channel_id=1, source_target_pairs={{0,48},{8,56},{16,0},{24,8},{32,16},{40,24},{48,32},{56,40},{64,11... | collective-permute-start | bytes 368648 | tf_op jit(solution)/shard_map/ppermute | solution.py:40
  179.4 2.4 %next_ring.3 = (f32[2,40,384]{2,1,0:T(8,128)}, f32[2,40,384]{2,1,0:T(8,128)}, f32[2,40,384]{2,1,0:T(8,128)}, f32[2,40,384]{2,1,0:T(8,128)}) custom-call(s32[5]{0:T(128)} %stack.39.edge_ref, f32[2,160,384]{2,1,0:T(8,128)} %get-tuple-element.96.own_in, f32[2,160,384]{2,1,0:T(8,128)} %copy-done.2, f32[2,160,384]{2,1,0:T(8,128)} %copy-done.4, ...), custom_call_target="tpu_custom_call" | custom-call | tf_op jit(solution)/shard_map/next_ring/pallas_call | solution.py:862
  181.9 3.5 %collective-permute-start.20 = (f32[2,40,384]{2,1,0:T(8,128)}, f32[2,40,384]{2,1,0:T(8,128)S(1)}, u32[]{:S(2)}, u32[]{:S(2)}) collective-permute-start(f32[2,40,384]{2,1,0:T(8,128)} %get-tuple-element.103), channel_id=1, source_target_pairs={{0,48},{8,56},{16,0},{24,8},{32,16},{40,24},{48,32},{56,40},{64,11... | collective-permute-start | bytes 368648 | tf_op jit(solution)/shard_map/ppermute | solution.py:40
  185.4 8.5 %collective-permute-done.13.from_below_ref.refs_1_ = f32[2,40,384]{2,1,0:T(8,128)S(1)} collective-permute-done((f32[2,40,384]{2,1,0:T(8,128)}, f32[2,40,384]{2,1,0:T(8,128)S(1)}, u32[]{:S(2)}, u32[]{:S(2)}) %collective-permute-start.13) | collective-permute-done | bytes 122912 | tf_op jit(solution)/shard_map/ppermute | solution.py:40
  194.5 1.7 pass_on.6
  196.5 3.3 %collective-permute-start.18 = (f32[40,384]{1,0:T(8,128)}, f32[40,384]{1,0:T(8,128)S(1)}, u32[]{:S(2)}, u32[]{:S(2)}) collective-permute-start(f32[40,384]{1,0:T(8,128)} %get-tuple-element.100), channel_id=1, source_target_pairs={{0,48},{8,56},{16,0},{24,8},{32,16},{40,24},{48,32},{56,40},{64,11... | collective-permute-start | bytes 184328 | tf_op jit(solution)/shard_map/ppermute | solution.py:40
  201.1 1.7 pass_on.7
  203.1 3.2 %collective-permute-start.22 = (f32[40,384]{1,0:T(8,128)}, f32[40,384]{1,0:T(8,128)S(1)}, u32[]{:S(2)}, u32[]{:S(2)}) collective-permute-start(f32[40,384]{1,0:T(8,128)} %get-tuple-element.105), channel_id=1, source_target_pairs={{0,48},{8,56},{16,0},{24,8},{32,16},{40,24},{48,32},{56,40},{64,11... | collective-permute-start | bytes 184328 | tf_op jit(solution)/shard_map/ppermute | solution.py:40
  206.4 1.8 collective-permute-done.21.refs_8_
  208.2 1.4 collective-permute-done.22.refs_9_
  210.2 2.0 last_ring.1
  212.2 3.4 %token_sum.1 = bf16[320,512]{1,0:T(8,128)(2,1)} custom-call(f32[8,320,512]{2,1,0:T(8,128)} %all-to-all-done.2.parts_ref), custom_call_target="tpu_custom_call" | custom-call | tf_op jit(solution)/shard_map/token_sum/pallas_call | solution.py:920
  (82 shorter events, 15.3 us)
Async XLA Ops:
  1.4 6.3 %collective-permute-start = (f32[8,2560]{1,0:T(8,128)S(1)}, f32[8,2560]{1,0:T(8,128)S(1)}, u32[]{:S(2)}, u32[]{:S(2)}) collective-permute-start(f32[8,2560]{1,0:T(8,128)S(1)} %slice_convert_fusion), channel_id=1, source_target_pairs={{0,8},{8,16},{16,24},{24,32},{32,40},{40,48},{48,56},{56,64},{64,7... | collective-permute-start | bytes 245768 | tf_op jit(solution)/shard_map/ppermute | solution.py:27
  21.6 7.2 %collective-permute-start.1 = (f32[16,48,128]{2,1,0:T(8,128)}, f32[16,48,128]{2,1,0:T(8,128)S(1)}, u32[]{:S(2)}, u32[]{:S(2)}) collective-permute-start(f32[16,48,128]{2,1,0:T(8,128)} %get-tuple-element.67.send_ref), channel_id=1, source_target_pairs={{0,8},{8,0},{16,24},{24,16},{32,40},{40,32},{48,56},{56,48},{64,72... | collective-permute-start | bytes 1179656 | tf_op jit(solution)/shard_map/ppermute | solution.py:40
  28.8 0.7 copy-start.13
  31.5 20.3 %all-to-all-start = ((f32[16,48,128]{2,1,0:T(8,128)}), f32[16,48,128]{2,1,0:T(8,128)S(1)}, u32[]{:S(2)}, u32[]{:S(2)}) async-start(f32[16,48,128]{2,1,0:T(8,128)} %chip_state.1), calls=%async_computation | async-start | bytes 786432 | tf_op jit(solution)/shard_map/all_to_all | solution.py:651
  51.8 0.7 copy-start.6
  77.3 4.3 %collective-permute-start.2 = (f32[16,40,128]{2,1,0:T(8,128)}, f32[16,40,128]{2,1,0:T(8,128)S(1)}, u32[]{:S(2)}, u32[]{:S(2)}) collective-permute-start(f32[16,40,128]{2,1,0:T(8,128)} %onward.1), channel_id=1, source_target_pairs={{0,8},{8,0},{16,24},{24,16},{32,40},{40,32},{48,56},{56,48},{64,72... | collective-permute-start | bytes 983048 | tf_op jit(solution)/shard_map/ppermute | solution.py:40
  81.6 0.7 copy-start.14
  92.4 4.5 %collective-permute-start.3 = (f32[8,896]{1,0:T(8,128)}, f32[8,896]{1,0:T(8,128)S(1)}, u32[]{:S(2)}, u32[]{:S(2)}) collective-permute-start(f32[8,896]{1,0:T(8,128)} %get-tuple-element.71), channel_id=1, source_target_pairs={{0,248},{8,0},{16,8},{24,16},{32,24},{40,32},{48,40},{56,48},{64,5... | collective-permute-start | bytes 86024 | tf_op jit(solution)/shard_map/ppermute | solution.py:27
  101.3 19.7 %all-to-all-start.3 = ((f32[8,32,512]{2,1,0:T(8,128)}), f32[8,32,512]{2,1,0:T(8,128)S(1)}, u32[]{:S(2)}, u32[]{:S(2)}) async-start(f32[8,32,512]{2,1,0:T(8,128)} %bitcast.13), calls=%async_computation.3 | async-start | bytes 1048576 | tf_op jit(solution)/shard_map/all_to_all | solution.py:785
  121.1 0.8 copy-start
  121.9 90.3 %all-to-all-start.2 = ((f32[8,320,512]{2,1,0:T(8,128)}), f32[8,320,512]{2,1,0:T(8,128)}, u32[]{:S(2)}, u32[]{:S(2)}) async-start(f32[8,320,512]{2,1,0:T(8,128)} %token_grad.1.refs_2_), calls=%async_computation.2 | async-start | bytes 10485760 | tf_op jit(solution)/shard_map/all_to_all | solution.py:835
  127.0 4.2 %collective-permute-start.4 = (f32[4,2,160,384]{3,2,1,0:T(8,128)}, f32[4,2,160,384]{3,2,1,0:T(8,128)S(1)}, u32[]{:S(2)}, u32[]{:S(2)}) collective-permute-start(f32[4,2,160,384]{3,2,1,0:T(8,128)} %get-tuple-element.76), channel_id=1, source_target_pairs={{0,8},{8,0},{16,24},{24,16},{32,40},{40,32},{48,56},{56,48},{64,72... | collective-permute-start | bytes 5898248 | tf_op jit(solution)/shard_map/ppermute | solution.py:40
  127.0 16.9 %collective-permute-start.7 = (f32[4,2,160,256]{3,2,1,0:T(8,128)}, f32[4,2,160,256]{3,2,1,0:T(8,128)S(1)}, u32[]{:S(2)}, u32[]{:S(2)}) collective-permute-start(f32[4,2,160,256]{3,2,1,0:T(8,128)} %get-tuple-element.82), channel_id=1, source_target_pairs={{0,8},{8,0},{16,24},{24,16},{32,40},{40,32},{48,56},{56,48},{64,72... | collective-permute-start | bytes 3932168 | tf_op jit(solution)/shard_map/ppermute | solution.py:40
  131.2 1.3 copy-start.1
  136.1 5.2 %copy-start.26 = (f32[2,160,384]{2,1,0:T(8,128)S(1)}, f32[2,160,384]{2,1,0:T(8,128)}, u32[]{:S(2)}) copy-start(f32[2,160,384]{2,1,0:T(8,128)} %get-tuple-element.78) | copy-start | bytes 1474564
  136.1 5.5 %copy-start.25 = (f32[2,160,384]{2,1,0:T(8,128)S(1)}, f32[2,160,384]{2,1,0:T(8,128)}, u32[]{:S(2)}) copy-start(f32[2,160,384]{2,1,0:T(8,128)} %get-tuple-element.79) | copy-start | bytes 1474564
  141.2 2.8 %collective-permute-start.8 = (f32[4,2,160,128]{3,2,1,0:T(8,128)}, f32[4,2,160,128]{3,2,1,0:T(8,128)S(1)}, u32[]{:S(2)}, u32[]{:S(2)}) collective-permute-start(f32[4,2,160,128]{3,2,1,0:T(8,128)} %get-tuple-element.85), channel_id=1, source_target_pairs={{0,8},{8,0},{16,24},{24,16},{32,40},{40,32},{48,56},{56,48},{64,72... | collective-permute-start | bytes 1966088 | tf_op jit(solution)/shard_map/ppermute | solution.py:40
  141.3 13.7 %collective-permute-start.5 = (f32[2,160,384]{2,1,0:T(8,128)S(1)}, f32[2,160,384]{2,1,0:T(8,128)S(1)}, u32[]{:S(2)}, u32[]{:S(2)}) collective-permute-start(f32[2,160,384]{2,1,0:T(8,128)S(1)} %copy-done.26), channel_id=1, source_target_pairs={{0,64},{8,72},{16,80},{24,88},{32,96},{40,104},{48,112},{56,120},{... | collective-permute-start | bytes 1474568 | tf_op jit(solution)/shard_map/ppermute | solution.py:40
  141.5 13.4 %collective-permute-start.6 = (f32[2,160,384]{2,1,0:T(8,128)S(1)}, f32[2,160,384]{2,1,0:T(8,128)S(1)}, u32[]{:S(2)}, u32[]{:S(2)}) collective-permute-start(f32[2,160,384]{2,1,0:T(8,128)S(1)} %copy-done.25), channel_id=1, source_target_pairs={{0,192},{8,200},{16,208},{24,216},{32,224},{40,232},{48,240},{56,2... | collective-permute-start | bytes 1474568 | tf_op jit(solution)/shard_map/ppermute | solution.py:40
  144.0 1.1 copy-start.7
  144.0 1.3 copy-start.8
  148.8 16.7 %collective-permute-start.11 = (f32[2,160,384]{2,1,0:T(8,128)}, f32[2,160,384]{2,1,0:T(8,128)S(1)}, u32[]{:S(2)}, u32[]{:S(2)}) collective-permute-start(f32[2,160,384]{2,1,0:T(8,128)} %get-tuple-element.89), channel_id=1, source_target_pairs={{0,64},{8,72},{16,80},{24,88},{32,96},{40,104},{48,112},{56,120},{... | collective-permute-start | bytes 1474568 | tf_op jit(solution)/shard_map/ppermute | solution.py:40
  148.8 16.7 %collective-permute-start.12 = (f32[2,160,384]{2,1,0:T(8,128)}, f32[2,160,384]{2,1,0:T(8,128)S(1)}, u32[]{:S(2)}, u32[]{:S(2)}) collective-permute-start(f32[2,160,384]{2,1,0:T(8,128)} %get-tuple-element.90), channel_id=1, source_target_pairs={{0,192},{8,200},{16,208},{24,216},{32,224},{40,232},{48,240},{56,2... | collective-permute-start | bytes 1474568 | tf_op jit(solution)/shard_map/ppermute | solution.py:40
  155.0 0.8 copy-start.3
  155.0 1.0 copy-start.5
  158.2 13.8 %collective-permute-start.10 = (f32[160,384]{1,0:T(8,128)}, f32[160,384]{1,0:T(8,128)S(1)}, u32[]{:S(2)}, u32[]{:S(2)}) collective-permute-start(f32[160,384]{1,0:T(8,128)} %get-tuple-element.88), channel_id=1, source_target_pairs={{0,192},{8,200},{16,208},{24,216},{32,224},{40,232},{48,240},{56,2... | collective-permute-start | bytes 737288 | tf_op jit(solution)/shard_map/ppermute | solution.py:40
  160.3 11.6 %collective-permute-start.9 = (f32[160,384]{1,0:T(8,128)}, f32[160,384]{1,0:T(8,128)S(1)}, u32[]{:S(2)}, u32[]{:S(2)}) collective-permute-start(f32[160,384]{1,0:T(8,128)} %get-tuple-element.87.after_ref), channel_id=1, source_target_pairs={{0,64},{8,72},{16,80},{24,88},{32,96},{40,104},{48,112},{56,120},{... | collective-permute-start | bytes 737288 | tf_op jit(solution)/shard_map/ppermute | solution.py:40
  165.5 0.8 copy-start.2
  166.3 0.8 copy-start.4
  169.2 9.4 %collective-permute-start.15 = (f32[160,384]{1,0:T(8,128)}, f32[160,384]{1,0:T(8,128)S(1)}, u32[]{:S(2)}, u32[]{:S(2)}) collective-permute-start(f32[160,384]{1,0:T(8,128)} %get-tuple-element.91.after_ref), channel_id=1, source_target_pairs={{0,64},{8,72},{16,80},{24,88},{32,96},{40,104},{48,112},{56,120},{... | collective-permute-start | bytes 737288 | tf_op jit(solution)/shard_map/ppermute | solution.py:40
  169.2 9.4 %collective-permute-start.16 = (f32[160,384]{1,0:T(8,128)}, f32[160,384]{1,0:T(8,128)S(1)}, u32[]{:S(2)}, u32[]{:S(2)}) collective-permute-start(f32[160,384]{1,0:T(8,128)} %get-tuple-element.97), channel_id=1, source_target_pairs={{0,192},{8,200},{16,208},{24,216},{32,224},{40,232},{48,240},{56,2... | collective-permute-start | bytes 737288 | tf_op jit(solution)/shard_map/ppermute | solution.py:40
  171.9 0.7 copy-start.17
  171.9 0.8 copy-start.18
  175.0 18.8 %collective-permute-start.13 = (f32[2,40,384]{2,1,0:T(8,128)}, f32[2,40,384]{2,1,0:T(8,128)S(1)}, u32[]{:S(2)}, u32[]{:S(2)}) collective-permute-start(f32[2,40,384]{2,1,0:T(8,128)} %get-tuple-element.93), channel_id=1, source_target_pairs={{0,16},{8,24},{16,32},{24,40},{32,48},{40,56},{48,0},{56,8},{64,80... | collective-permute-start | bytes 368648 | tf_op jit(solution)/shard_map/ppermute | solution.py:40
  176.3 17.5 %collective-permute-start.14 = (f32[2,40,384]{2,1,0:T(8,128)}, f32[2,40,384]{2,1,0:T(8,128)S(1)}, u32[]{:S(2)}, u32[]{:S(2)}) collective-permute-start(f32[2,40,384]{2,1,0:T(8,128)} %get-tuple-element.94), channel_id=1, source_target_pairs={{0,48},{8,56},{16,0},{24,8},{32,16},{40,24},{48,32},{56,40},{64,11... | collective-permute-start | bytes 368648 | tf_op jit(solution)/shard_map/ppermute | solution.py:40
  178.6 0.7 copy-start.15
  178.6 0.8 copy-start.16
  181.8 18.0 %collective-permute-start.19 = (f32[2,40,384]{2,1,0:T(8,128)}, f32[2,40,384]{2,1,0:T(8,128)S(1)}, u32[]{:S(2)}, u32[]{:S(2)}) collective-permute-start(f32[2,40,384]{2,1,0:T(8,128)} %get-tuple-element.102), channel_id=1, source_target_pairs={{0,16},{8,24},{16,32},{24,40},{32,48},{40,56},{48,0},{56,8},{64,80... | collective-permute-start | bytes 368648 | tf_op jit(solution)/shard_map/ppermute | solution.py:40
  181.9 17.9 %collective-permute-start.20 = (f32[2,40,384]{2,1,0:T(8,128)}, f32[2,40,384]{2,1,0:T(8,128)S(1)}, u32[]{:S(2)}, u32[]{:S(2)}) collective-permute-start(f32[2,40,384]{2,1,0:T(8,128)} %get-tuple-element.103), channel_id=1, source_target_pairs={{0,48},{8,56},{16,0},{24,8},{32,16},{40,24},{48,32},{56,40},{64,11... | collective-permute-start | bytes 368648 | tf_op jit(solution)/shard_map/ppermute | solution.py:40
  193.9 0.7 copy-start.10
  196.2 10.1 %collective-permute-start.17 = (f32[40,384]{1,0:T(8,128)}, f32[40,384]{1,0:T(8,128)S(1)}, u32[]{:S(2)}, u32[]{:S(2)}) collective-permute-start(f32[40,384]{1,0:T(8,128)} %get-tuple-element.99.after_ref), channel_id=1, source_target_pairs={{0,16},{8,24},{16,32},{24,40},{32,48},{40,56},{48,0},{56,8},{64,80... | collective-permute-start | bytes 184328 | tf_op jit(solution)/shard_map/ppermute | solution.py:40
  196.5 9.9 %collective-permute-start.18 = (f32[40,384]{1,0:T(8,128)}, f32[40,384]{1,0:T(8,128)S(1)}, u32[]{:S(2)}, u32[]{:S(2)}) collective-permute-start(f32[40,384]{1,0:T(8,128)} %get-tuple-element.100), channel_id=1, source_target_pairs={{0,48},{8,56},{16,0},{24,8},{32,16},{40,24},{48,32},{56,40},{64,11... | collective-permute-start | bytes 184328 | tf_op jit(solution)/shard_map/ppermute | solution.py:40
  199.8 0.7 copy-start.11
  202.8 5.4 %collective-permute-start.21 = (f32[40,384]{1,0:T(8,128)}, f32[40,384]{1,0:T(8,128)S(1)}, u32[]{:S(2)}, u32[]{:S(2)}) collective-permute-start(f32[40,384]{1,0:T(8,128)} %get-tuple-element.104), channel_id=1, source_target_pairs={{0,16},{8,24},{16,32},{24,40},{32,48},{40,56},{48,0},{56,8},{64,80... | collective-permute-start | bytes 184328 | tf_op jit(solution)/shard_map/ppermute | solution.py:40
  203.1 6.5 %collective-permute-start.22 = (f32[40,384]{1,0:T(8,128)}, f32[40,384]{1,0:T(8,128)S(1)}, u32[]{:S(2)}, u32[]{:S(2)}) collective-permute-start(f32[40,384]{1,0:T(8,128)} %get-tuple-element.105), channel_id=1, source_target_pairs={{0,48},{8,56},{16,0},{24,8},{32,16},{40,24},{48,32},{56,40},{64,11... | collective-permute-start | bytes 184328 | tf_op jit(solution)/shard_map/ppermute | solution.py:40
  206.3 3.3 %copy-start.20 = (f32[40,384]{1,0:T(8,128)}, f32[40,384]{1,0:T(8,128)S(1)}, u32[]{:S(2)}) copy-start(f32[40,384]{1,0:T(8,128)S(1)} %collective-permute-done.17.refs_3_) | copy-start | bytes 184324
  206.4 3.3 %copy-start.21 = (f32[40,384]{1,0:T(8,128)}, f32[40,384]{1,0:T(8,128)S(1)}, u32[]{:S(2)}) copy-start(f32[40,384]{1,0:T(8,128)S(1)} %collective-permute-done.18.refs_4_) | copy-start | bytes 184324
  208.2 1.4 copy-start.22
  (5 other events, 3.2 us)
